TPU v7x, 256 devices: a whole 4x4x8 slice. The times are simulated.
256 devices in a mesh: ctx: 32 (over x, z_hi, core), chan: 8 (over y, z_lo).
Axes of the slice: x: 4, y: 4, z: 8 (z_hi: 4, z_lo: 2; z = z_hi * 2 + z_lo), core: 2. Of those that a mesh axis runs over, the one named last changes fastest.
Arguments:
- grad_out: bfloat16 [256, 32768], P('chan', 'ctx'), may hold values from -6 to 6
- query: bfloat16 [256, 32768], P('chan', 'ctx'), may hold values from -6 to 6
- key_proj: bfloat16 [256, 32768], P('chan', 'ctx'), may hold values from -6 to 6
- value: bfloat16 [256, 32768], P('chan', 'ctx'), may hold values from -6 to 6
- filter_param: float32 [32, 32768], P(None, 'ctx'), may hold values from -6 to 6
Outputs:
- grad_query: bfloat16 [256, 32768], P('chan', 'ctx')
- grad_key: bfloat16 [256, 32768], P('chan', 'ctx')
- grad_value: bfloat16 [256, 32768], P('chan', 'ctx')
- grad_filter: float32 [32, 32768], P(None, 'ctx')
All inputs are finite; a program needn't handle non-finite values.
Results may differ from a plain program's by a relative error of at most 0.004.
Values sent between devices are 32-bit elements; how exact they have to be, the bound alone decides.
No kernel may reach another device: no remote copies, remote signals or barrier semaphores. Data moves between devices by JAX's collectives and lax.ppermute only.
A program may use at most 128 MiB of HBM per device.

v0:
```python
import math

import jax
import jax.numpy as jnp
import ml_dtypes
import numpy as np
from jax import lax
from jax.experimental import pallas as pl
from jax.experimental.pallas import tpu as pltpu
from jax.sharding import PartitionSpec as P

LANES = 128
SUBLANES = 8


def split_table(table):
    high = table.astype(np.float32).astype(ml_dtypes.bfloat16)
    low = (table - high.astype(np.float64)).astype(ml_dtypes.bfloat16)
    return high, low


def transform_tables(tokens):
    length = 2 * tokens
    rows = length // LANES
    half = rows // 2
    k1 = np.arange(half, dtype=np.float64) + 0.5
    n1 = np.arange(half, dtype=np.float64)
    n2 = np.arange(LANES, dtype=np.float64)
    outer = 2.0 * np.pi * k1[:, None] * n1[None, :] / rows
    first = np.concatenate([np.cos(outer), -np.sin(outer)], axis=0)
    last = first.T * (2.0 / length)
    twist = 2.0 * np.pi * k1[:, None] * n2[None, :] / length
    twist_cos = np.cos(twist).astype(np.float32)
    twist_sin = (-np.sin(twist)).astype(np.float32)
    inner = 2.0 * np.pi * n2[:, None] * n2[None, :] / LANES
    cos, sin = np.cos(inner), np.sin(inner)
    ahead = np.block([[cos, -sin], [sin, cos]])
    back = np.block([[cos, sin], [-sin, cos]])
    return split_table(first) + split_table(ahead) + split_table(back) + split_table(last) + (twist_cos, twist_sin)


def gate_kernel(grad_out, query, key_proj, value, filter_param, out, *, filter_scale):
    f32 = jnp.float32
    channels, here = key_proj.shape
    pieces = here // LANES
    stride = 3 * pieces
    parts = (
        key_proj[...].astype(f32) * value[...].astype(f32),
        grad_out[...].astype(f32) * query[...].astype(f32),
        filter_param[...] * filter_scale,
    )
    for index, part in enumerate(parts):
        for piece in range(pieces):
            out[pl.ds(index * pieces + piece, channels, stride=stride), :] = part[:, piece * LANES : (piece + 1) * LANES]


def split(values):
    high = values.astype(jnp.bfloat16)
    low = (values - high.astype(jnp.float32)).astype(jnp.bfloat16)
    return high, low


def product(left, right):
    def dot(a, b):
        return jnp.dot(a, b, preferred_element_type=jnp.float32)

    return dot(left[0], right[0]) + (dot(left[0], right[1]) + dot(left[1], right[0]))


def spectral_kernel(
    taken, first_h, first_l, ahead_h, ahead_l, back_h, back_l, last_h, last_l, twist_cos, twist_sin, out, *, filter_scale
):
    shards = taken.shape[0]
    pieces = taken.shape[1] // 3
    half = shards * pieces
    cos, sin = twist_cos[...], twist_sin[...]
    stacked = jnp.concatenate(
        [taken[:, i * pieces : (i + 1) * pieces, :].reshape(half, LANES) for i in range(3)], axis=1
    )
    mixed = product((first_h[...], first_l[...]), split(stacked))
    specs = []
    for i in range(3):
        real, imag = mixed[:half, i * LANES : (i + 1) * LANES], mixed[half:, i * LANES : (i + 1) * LANES]
        turned = jnp.concatenate([real * cos - imag * sin, real * sin + imag * cos], axis=1)
        spec = product(split(turned), (ahead_h[...], ahead_l[...]))
        specs.append((spec[:, :LANES], spec[:, LANES:]))
    (sig_re, sig_im), (cot_re, cot_im), (filt_re, filt_im) = specs
    results = (
        (filt_re * sig_re - filt_im * sig_im, filt_re * sig_im + filt_im * sig_re),
        (filt_re * cot_re + filt_im * cot_im, filt_re * cot_im - filt_im * cot_re),
        (
            (cot_re * sig_re + cot_im * sig_im) * filter_scale,
            (cot_im * sig_re - cot_re * sig_im) * filter_scale,
        ),
    )
    columns = []
    for result in results:
        spec = product(split(jnp.concatenate(result, axis=1)), (back_h[...], back_l[...]))
        real, imag = spec[:, :LANES], spec[:, LANES:]
        columns.append(jnp.concatenate([real * cos + imag * sin, imag * cos - real * sin], axis=0))
    timed = product((last_h[...], last_l[...]), split(jnp.concatenate(columns, axis=1)))
    for i in range(3):
        out[:, i * pieces : (i + 1) * pieces, :] = timed[:, i * LANES : (i + 1) * LANES].reshape(shards, pieces, LANES)


def grads_kernel(back, grad_out, key_proj, value, grad_query, grad_key, grad_value):
    f32 = jnp.float32
    channels, here = key_proj.shape
    pieces = here // LANES
    stride = 3 * pieces
    for piece in range(pieces):
        columns = slice(piece * LANES, (piece + 1) * LANES)
        conv = back[pl.ds(piece, channels, stride=stride), :]
        grad_signal = back[pl.ds(pieces + piece, channels, stride=stride), :]
        grad_query[:, columns] = (grad_out[:, columns].astype(f32) * conv).astype(jnp.bfloat16)
        grad_key[:, columns] = (grad_signal * value[:, columns].astype(f32)).astype(jnp.bfloat16)
        grad_value[:, columns] = (grad_signal * key_proj[:, columns].astype(f32)).astype(jnp.bfloat16)


def total_kernel(first, second, third, fourth, out):
    channels, here = out.shape
    pieces = here // LANES
    for piece in range(pieces):
        rows = pl.ds(piece, channels, stride=pieces)
        out[:, piece * LANES : (piece + 1) * LANES] = (first[rows, :] + second[rows, :]) + (third[rows, :] + fourth[rows, :])


def local(grad_out, query, key_proj, value, filter_param):
    f32 = jnp.float32
    shards = lax.axis_size("ctx")
    groups = lax.axis_size("chan")
    channels, here = grad_out.shape
    tokens = shards * here
    pieces = here // LANES
    filter_scale = 1.0 / math.sqrt(tokens)
    params = pltpu.CompilerParams(vmem_limit_bytes=24 * 1024 * 1024)
    gated = pl.pallas_call(
        lambda *refs: gate_kernel(*refs, filter_scale=filter_scale),
        out_shape=jax.ShapeDtypeStruct((channels * 3 * pieces, LANES), f32),
        compiler_params=params,
        name="gate",
    )(grad_out, query, key_proj, value, filter_param)
    taken = lax.all_to_all(gated.reshape(channels, 3 * pieces, LANES), "ctx", 0, 0, tiled=True)
    tables = [jnp.asarray(table) for table in transform_tables(tokens)]
    timed = pl.pallas_call(
        lambda *refs: spectral_kernel(*refs, filter_scale=filter_scale),
        out_shape=jax.ShapeDtypeStruct((shards, 3 * pieces, LANES), f32),
        compiler_params=params,
        name="spectral",
    )(taken, *tables)
    back = lax.all_to_all(timed, "ctx", 0, 0, tiled=True)
    partial = back[:, 2 * pieces :, :].reshape(channels * pieces, LANES)
    pair = partial + lax.ppermute(partial, "chan", [(i, i ^ 1) for i in range(groups)])
    others = [
        lax.ppermute(pair, "chan", [(i, (i + 2 * step) % groups) for i in range(groups)]) for step in range(1, groups // 2)
    ]
    grad_query, grad_key, grad_value = pl.pallas_call(
        grads_kernel,
        out_shape=[jax.ShapeDtypeStruct((channels, here), jnp.bfloat16)] * 3,
        compiler_params=params,
        name="grads",
    )(back.reshape(channels * 3 * pieces, LANES), grad_out, key_proj, value)
    grad_filter = pl.pallas_call(
        total_kernel,
        out_shape=jax.ShapeDtypeStruct((channels, here), f32),
        compiler_params=params,
        name="total",
    )(pair, *others)
    return (grad_query, grad_key, grad_value, grad_filter)


def solution(mesh):
    split_spec = P("chan", "ctx")
    in_specs = (split_spec, split_spec, split_spec, split_spec, P(None, "ctx"))
    out_specs = (split_spec, split_spec, split_spec, P(None, "ctx"))
    return jax.shard_map(local, mesh=mesh, in_specs=in_specs, out_specs=out_specs, check_vma=False)
```

profile of v0, /device:TPU:32, one launch (start us, length us, event | category | flops | bytes accessed | tf_op | source)
XLA Modules:
  0.0 72.4 jit_solution(16199918595189832052)
XLA Ops:
  0.6 0.8 %copy-done.4 = bf16[32,1024]{1,0:T(8,128)(2,1)S(1)} copy-done((bf16[32,1024]{1,0:T(8,128)(2,1)S(1)}, bf16[32,1024]{1,0:T(8,128)(2,1)}, u32[]{:S(2)}) %copy-start.4) | copy-done | bytes 65560
  1.5 0.8 %copy-done.6 = bf16[32,1024]{1,0:T(8,128)(2,1)S(1)} copy-done((bf16[32,1024]{1,0:T(8,128)(2,1)S(1)}, bf16[32,1024]{1,0:T(8,128)(2,1)}, u32[]{:S(2)}) %copy-start.6) | copy-done | bytes 65560
  2.3 0.8 %copy-done.8 = bf16[32,1024]{1,0:T(8,128)(2,1)S(1)} copy-done((bf16[32,1024]{1,0:T(8,128)(2,1)S(1)}, bf16[32,1024]{1,0:T(8,128)(2,1)}, u32[]{:S(2)}) %copy-start.8) | copy-done | bytes 65560
  3.2 0.9 %copy-done.16 = f32[32,1024]{1,0:T(8,128)S(1)} copy-done((f32[32,1024]{1,0:T(8,128)S(1)}, f32[32,1024]{1,0:T(8,128)}, u32[]{:S(2)}) %copy-start.16) | copy-done | bytes 131096
  4.1 0.8 %copy-done.17 = bf16[32,1024]{1,0:T(8,128)(2,1)S(1)} copy-done((bf16[32,1024]{1,0:T(8,128)(2,1)S(1)}, bf16[32,1024]{1,0:T(8,128)(2,1)}, u32[]{:S(2)}) %copy-start.17) | copy-done | bytes 65560
  4.9 0.0 copy-start.13
  4.9 0.1 gate.1
  5.0 0.0 copy-start
  5.0 0.0 copy-start.1
  5.0 0.0 copy-start.2
  5.0 26.7 %all_to_all.10.refs_0_ = f32[32,24,128]{2,1,0:T(8,128)S(1)} all-to-all(f32[32,24,128]{2,1,0:T(8,128)S(1)} %bitcast.7), channel_id=1, replica_groups=mesh['ctx'=32,'chan'=8] {'ctx'}, dimensions={0} | all-to-all | bytes 786432 | tf_op jit(solution)/shard_map/all_to_all | solution.py:143
  31.8 0.0 copy-start.14
  31.9 0.9 %copy-done.14 = f32[256,128]{1,0:T(8,128)S(1)} copy-done((f32[256,128]{1,0:T(8,128)S(1)}, f32[256,128]{1,0:T(8,128)}, u32[]{:S(2)}) %copy-start.14) | copy-done | bytes 131096
  32.7 0.9 %copy-done.15 = f32[256,128]{1,0:T(8,128)S(1)} copy-done((f32[256,128]{1,0:T(8,128)S(1)}, f32[256,128]{1,0:T(8,128)}, u32[]{:S(2)}) %copy-start.15) | copy-done | bytes 131096
  33.7 2.1 %spectral.1 = f32[32,24,128]{2,1,0:T(8,128)S(1)} custom-call(f32[32,24,128]{2,1,0:T(8,128)S(1)} %all_to_all.10.refs_0_, bf16[512,256]{1,0:T(8,128)(2,1)S(1)} %copy-done, bf16[512,256]{1,0:T(8,128)(2,1)S(1)} %copy-done.1, bf16[256,256]{1,0:T(8,128)(2,1)S(1)} %copy-done.10, bf16[256,256]{1,0:T(8,128)(2,1)S(1)} %copy-done.11, bf16[256,256]{1,0:T(8,128)(2,1)S(1)} %copy-done.12, ...), custom_call_target="tpu_custom_call" | custom-call | tf_op jit(solution)/shard_map/spectral/pallas_call | solution.py:145
  35.8 19.5 %all_to_all.11 = f32[32,24,128]{2,1,0:T(8,128)S(1)} all-to-all(f32[32,24,128]{2,1,0:T(8,128)S(1)} %spectral.1), channel_id=1, replica_groups=mesh['ctx'=32,'chan'=8] {'ctx'}, dimensions={0} | all-to-all | bytes 786432 | tf_op jit(solution)/shard_map/all_to_all | solution.py:151
  55.3 1.1 %collective-permute-start = (f32[256,128]{1,0:T(8,128)S(1)}, f32[256,128]{1,0:T(8,128)S(1)}, u32[]{:S(2)}, u32[]{:S(2)}) collective-permute-start(f32[256,128]{1,0:T(8,128)S(1)} %slice_bitcast_fusion), channel_id=1, source_target_pairs={{0,1},{1,0},{2,3},{3,2},{4,5},{5,4},{6,7},{7,6},{8,9},{9,8},{10,11... | collective-permute-start | bytes 393224 | tf_op jit(solution)/shard_map/ppermute | solution.py:153
  56.4 4.8 %collective-permute-done = f32[256,128]{1,0:T(8,128)S(1)} collective-permute-done((f32[256,128]{1,0:T(8,128)S(1)}, f32[256,128]{1,0:T(8,128)S(1)}, u32[]{:S(2)}, u32[]{:S(2)}) %collective-permute-start) | collective-permute-done | bytes 131104 | tf_op jit(solution)/shard_map/ppermute | solution.py:153
  61.3 1.7 %collective-permute-start.1 = (f32[256,128]{1,0:T(8,128)S(1)}, f32[256,128]{1,0:T(8,128)S(1)}, u32[]{:S(2)}, u32[]{:S(2)}) collective-permute-start(f32[256,128]{1,0:T(8,128)S(1)} %fusion.first), channel_id=1, source_target_pairs={{0,2},{1,3},{2,4},{3,5},{4,6},{5,7},{6,0},{7,1},{8,10},{9,11},{10,... | collective-permute-start | bytes 393224 | tf_op jit(solution)/shard_map/ppermute | solution.py:155
  62.9 2.9 %collective-permute-start.2 = (f32[256,128]{1,0:T(8,128)S(1)}, f32[256,128]{1,0:T(8,128)S(1)}, u32[]{:S(2)}, u32[]{:S(2)}) collective-permute-start(f32[256,128]{1,0:T(8,128)S(1)} %fusion.first), channel_id=1, source_target_pairs={{0,4},{1,5},{2,6},{3,7},{4,0},{5,1},{6,2},{7,3},{8,12},{9,13},{10,... | collective-permute-start | bytes 393224 | tf_op jit(solution)/shard_map/ppermute | solution.py:155
  65.8 1.3 %collective-permute-start.3 = (f32[256,128]{1,0:T(8,128)S(1)}, f32[256,128]{1,0:T(8,128)S(1)}, u32[]{:S(2)}, u32[]{:S(2)}) collective-permute-start(f32[256,128]{1,0:T(8,128)S(1)} %fusion.first), channel_id=1, source_target_pairs={{0,6},{1,7},{2,0},{3,1},{4,2},{5,3},{6,4},{7,5},{8,14},{9,15},{10,... | collective-permute-start | bytes 393224 | tf_op jit(solution)/shard_map/ppermute | solution.py:155
  67.2 0.7 %grads.1 = (bf16[32,1024]{1,0:T(8,128)(2,1)}, bf16[32,1024]{1,0:T(8,128)(2,1)}, bf16[32,1024]{1,0:T(8,128)(2,1)}) custom-call(f32[768,128]{1,0:T(8,128)S(1)} %bitcast.6, bf16[32,1024]{1,0:T(8,128)(2,1)S(1)} %copy-done.5, bf16[32,1024]{1,0:T(8,128)(2,1)S(1)} %copy-done.7, bf16[32,1024]{1,0:T(8,128)(2,1)S(1)} %copy-done.9), custom_call_target="tpu_custom_call" | custom-call | tf_op jit(solution)/shard_map/grads/pallas_call | solution.py:157
  67.9 3.7 %collective-permute-done.2.third = f32[256,128]{1,0:T(8,128)S(1)} collective-permute-done((f32[256,128]{1,0:T(8,128)S(1)}, f32[256,128]{1,0:T(8,128)S(1)}, u32[]{:S(2)}, u32[]{:S(2)}) %collective-permute-start.2) | collective-permute-done | bytes 131104 | tf_op jit(solution)/shard_map/ppermute | solution.py:155
  71.7 0.7 %total.1 = f32[32,1024]{1,0:T(8,128)} custom-call(f32[256,128]{1,0:T(8,128)S(1)} %fusion.first, f32[256,128]{1,0:T(8,128)S(1)} %collective-permute-done.1.second, f32[256,128]{1,0:T(8,128)S(1)} %collective-permute-done.2.third, f32[256,128]{1,0:T(8,128)S(1)} %collective-permute-done.3.fourth), custom_call_target="tpu_custom_call" | custom-call | tf_op jit(solution)/shard_map/total/pallas_call | solution.py:163
  (28 shorter events, 0.1 us)
Async XLA Ops:
  0.6 0.8 %copy-start.4 = (bf16[32,1024]{1,0:T(8,128)(2,1)S(1)}, bf16[32,1024]{1,0:T(8,128)(2,1)}, u32[]{:S(2)}) copy-start(bf16[32,1024]{1,0:T(8,128)(2,1)} %grad_out.1) | copy-start | bytes 196612
  1.5 0.8 %copy-start.6 = (bf16[32,1024]{1,0:T(8,128)(2,1)S(1)}, bf16[32,1024]{1,0:T(8,128)(2,1)}, u32[]{:S(2)}) copy-start(bf16[32,1024]{1,0:T(8,128)(2,1)} %key_proj.1) | copy-start | bytes 196612
  2.3 0.8 %copy-start.8 = (bf16[32,1024]{1,0:T(8,128)(2,1)S(1)}, bf16[32,1024]{1,0:T(8,128)(2,1)}, u32[]{:S(2)}) copy-start(bf16[32,1024]{1,0:T(8,128)(2,1)} %value.1) | copy-start | bytes 196612
  3.2 0.9 %copy-start.16 = (f32[32,1024]{1,0:T(8,128)S(1)}, f32[32,1024]{1,0:T(8,128)}, u32[]{:S(2)}) copy-start(f32[32,1024]{1,0:T(8,128)} %refs_4_.2) | copy-start | bytes 393220
  4.1 0.8 %copy-start.17 = (bf16[32,1024]{1,0:T(8,128)(2,1)S(1)}, bf16[32,1024]{1,0:T(8,128)(2,1)}, u32[]{:S(2)}) copy-start(bf16[32,1024]{1,0:T(8,128)(2,1)} %refs_1_.2) | copy-start | bytes 196612
  4.9 26.9 %copy-start.3 = (bf16[256,512]{1,0:T(8,128)(2,1)S(1)}, bf16[256,512]{1,0:T(8,128)(2,1)}, u32[]{:S(2)}) copy-start(bf16[256,512]{1,0:T(8,128)(2,1)} %constant.27.clone.refs_8_) | copy-start | bytes 786436
  4.9 26.9 %copy-start.10 = (bf16[256,256]{1,0:T(8,128)(2,1)S(1)}, bf16[256,256]{1,0:T(8,128)(2,1)}, u32[]{:S(2)}) copy-start(bf16[256,256]{1,0:T(8,128)(2,1)} %constant.22.clone.refs_3_) | copy-start | bytes 393220
  4.9 26.9 %copy-start.11 = (bf16[256,256]{1,0:T(8,128)(2,1)S(1)}, bf16[256,256]{1,0:T(8,128)(2,1)}, u32[]{:S(2)}) copy-start(bf16[256,256]{1,0:T(8,128)(2,1)} %constant.23.clone.refs_4_) | copy-start | bytes 393220
  4.9 26.9 %copy-start.12 = (bf16[256,256]{1,0:T(8,128)(2,1)S(1)}, bf16[256,256]{1,0:T(8,128)(2,1)}, u32[]{:S(2)}) copy-start(bf16[256,256]{1,0:T(8,128)(2,1)} %constant.24.clone.refs_5_) | copy-start | bytes 393220
  4.9 26.9 %copy-start.13 = (bf16[256,256]{1,0:T(8,128)(2,1)S(1)}, bf16[256,256]{1,0:T(8,128)(2,1)}, u32[]{:S(2)}) copy-start(bf16[256,256]{1,0:T(8,128)(2,1)} %constant.25.clone.refs_6_) | copy-start | bytes 393220
  5.0 26.8 %copy-start = (bf16[512,256]{1,0:T(8,128)(2,1)S(1)}, bf16[512,256]{1,0:T(8,128)(2,1)}, u32[]{:S(2)}) copy-start(bf16[512,256]{1,0:T(8,128)(2,1)} %constant.20.clone.refs_1_) | copy-start | bytes 786436
  5.0 26.8 %copy-start.1 = (bf16[512,256]{1,0:T(8,128)(2,1)S(1)}, bf16[512,256]{1,0:T(8,128)(2,1)}, u32[]{:S(2)}) copy-start(bf16[512,256]{1,0:T(8,128)(2,1)} %constant.21.clone.refs_2_) | copy-start | bytes 786436
  5.0 26.8 %copy-start.2 = (bf16[256,512]{1,0:T(8,128)(2,1)S(1)}, bf16[256,512]{1,0:T(8,128)(2,1)}, u32[]{:S(2)}) copy-start(bf16[256,512]{1,0:T(8,128)(2,1)} %constant.26.clone.refs_7_) | copy-start | bytes 786436
  31.8 0.9 %copy-start.14 = (f32[256,128]{1,0:T(8,128)S(1)}, f32[256,128]{1,0:T(8,128)}, u32[]{:S(2)}) copy-start(f32[256,128]{1,0:T(8,128)} %constant.28.clone.refs_9_) | copy-start | bytes 393220
  32.7 0.9 %copy-start.15 = (f32[256,128]{1,0:T(8,128)S(1)}, f32[256,128]{1,0:T(8,128)}, u32[]{:S(2)}) copy-start(f32[256,128]{1,0:T(8,128)} %constant.29.clone.refs_10_) | copy-start | bytes 393220
  55.3 11.9 %copy-start.5 = (bf16[32,1024]{1,0:T(8,128)(2,1)S(1)}, bf16[32,1024]{1,0:T(8,128)(2,1)}, u32[]{:S(2)}) copy-start(bf16[32,1024]{1,0:T(8,128)(2,1)} %grad_out.1) | copy-start | bytes 196612
  55.3 11.9 %copy-start.7 = (bf16[32,1024]{1,0:T(8,128)(2,1)S(1)}, bf16[32,1024]{1,0:T(8,128)(2,1)}, u32[]{:S(2)}) copy-start(bf16[32,1024]{1,0:T(8,128)(2,1)} %key_proj.1) | copy-start | bytes 196612
  55.3 11.9 %copy-start.9 = (bf16[32,1024]{1,0:T(8,128)(2,1)S(1)}, bf16[32,1024]{1,0:T(8,128)(2,1)}, u32[]{:S(2)}) copy-start(bf16[32,1024]{1,0:T(8,128)(2,1)} %value.1) | copy-start | bytes 196612
  55.3 5.9 %collective-permute-start = (f32[256,128]{1,0:T(8,128)S(1)}, f32[256,128]{1,0:T(8,128)S(1)}, u32[]{:S(2)}, u32[]{:S(2)}) collective-permute-start(f32[256,128]{1,0:T(8,128)S(1)} %slice_bitcast_fusion), channel_id=1, source_target_pairs={{0,1},{1,0},{2,3},{3,2},{4,5},{5,4},{6,7},{7,6},{8,9},{9,8},{10,11... | collective-permute-start | bytes 393224 | tf_op jit(solution)/shard_map/ppermute | solution.py:153
  61.3 6.7 %collective-permute-start.1 = (f32[256,128]{1,0:T(8,128)S(1)}, f32[256,128]{1,0:T(8,128)S(1)}, u32[]{:S(2)}, u32[]{:S(2)}) collective-permute-start(f32[256,128]{1,0:T(8,128)S(1)} %fusion.first), channel_id=1, source_target_pairs={{0,2},{1,3},{2,4},{3,5},{4,6},{5,7},{6,0},{7,1},{8,10},{9,11},{10,... | collective-permute-start | bytes 393224 | tf_op jit(solution)/shard_map/ppermute | solution.py:155
  62.9 8.7 %collective-permute-start.2 = (f32[256,128]{1,0:T(8,128)S(1)}, f32[256,128]{1,0:T(8,128)S(1)}, u32[]{:S(2)}, u32[]{:S(2)}) collective-permute-start(f32[256,128]{1,0:T(8,128)S(1)} %fusion.first), channel_id=1, source_target_pairs={{0,4},{1,5},{2,6},{3,7},{4,0},{5,1},{6,2},{7,3},{8,12},{9,13},{10,... | collective-permute-start | bytes 393224 | tf_op jit(solution)/shard_map/ppermute | solution.py:155
  65.8 5.8 %collective-permute-start.3 = (f32[256,128]{1,0:T(8,128)S(1)}, f32[256,128]{1,0:T(8,128)S(1)}, u32[]{:S(2)}, u32[]{:S(2)}) collective-permute-start(f32[256,128]{1,0:T(8,128)S(1)} %fusion.first), channel_id=1, source_target_pairs={{0,6},{1,7},{2,0},{3,1},{4,2},{5,3},{6,4},{7,5},{8,14},{9,15},{10,... | collective-permute-start | bytes 393224 | tf_op jit(solution)/shard_map/ppermute | solution.py:155
where the time goes:
time: 72.8 us; the launch traced here: 72.4 us
  blocking collectives  46.2 us (63%)
  waiting for transfers between devices  8.56 us (12%)
  starting transfers between devices  7.01 us (10%)
  local copies, waits for them, and re-layouts  6.13 us (8%)
  Pallas kernels  3.69 us (5%)
  between operations  0.79 us (1%)
    all_to_all x1, blocking collectives, local(): lax.all_to_all(gated.reshape(channels, 3 * pieces, LANES), 'ctx', 0, 0, t...  26.7 us
    all_to_all x1, blocking collectives, local(): back = lax.all_to_all(timed, 'ctx', 0, 0, tiled=True)  19.5 us
    unnamed x36, local copies, waits for them, and re-layouts  6.12 us
    ppermute x3, starting transfers between devices, local(): lax.ppermute(pair, 'chan', [(i, (i + 2 * step) % groups) for i in range(g...  5.9 us
    ppermute x1, waiting for transfers between devices, local(): lax.ppermute(partial, 'chan', [(i, i ^ 1) for i in range(groups)])  4.82 us
    ppermute x3, waiting for transfers between devices, local(): lax.ppermute(pair, 'chan', [(i, (i + 2 * step) % groups) for i in range(g...  3.74 us
    pallas_call x1, Pallas kernels, local(): pl.pallas_call(lambda *refs: spectral_kernel(*refs, filter_scale=filter_s...  2.15 us
  transfers between devices with their start and end apart: 4, of which 2 were waited for; matrix products, arithmetic and copies ran while one was open for 0% of the time, Pallas kernels for 1%

commit v1 on v0

--- a/solution.py
+++ b/solution.py
@@ -27,31 +27,39 @@
     n1 = np.arange(half, dtype=np.float64)
     n2 = np.arange(LANES, dtype=np.float64)
     outer = 2.0 * np.pi * k1[:, None] * n1[None, :] / rows
-    first = np.concatenate([np.cos(outer), -np.sin(outer)], axis=0)
-    last = first.T * (2.0 / length)
+    cos, sin = np.cos(outer), np.sin(outer)
+    first = np.concatenate([cos, -sin], axis=0)
+    last = np.concatenate([cos.T, sin.T], axis=1) * (2.0 / length)
     twist = 2.0 * np.pi * k1[:, None] * n2[None, :] / length
-    twist_cos = np.cos(twist).astype(np.float32)
-    twist_sin = (-np.sin(twist)).astype(np.float32)
+    twists = np.concatenate([np.cos(twist), -np.sin(twist)], axis=1).astype(np.float32)
     inner = 2.0 * np.pi * n2[:, None] * n2[None, :] / LANES
     cos, sin = np.cos(inner), np.sin(inner)
-    ahead = np.block([[cos, -sin], [sin, cos]])
-    back = np.block([[cos, sin], [-sin, cos]])
-    return split_table(first) + split_table(ahead) + split_table(back) + split_table(last) + (twist_cos, twist_sin)
+    second = np.block([[cos, -sin], [sin, cos]])
+    return split_table(first) + split_table(second) + split_table(last) + (twists,)
 
 
-def gate_kernel(grad_out, query, key_proj, value, filter_param, out, *, filter_scale):
+def gate_kernel(grad_out, query, key_proj, value, filter_param, out, go, q, k, v, filt, sems, *, filter_scale):
     f32 = jnp.float32
     channels, here = key_proj.shape
     pieces = here // LANES
     stride = 3 * pieces
-    parts = (
-        key_proj[...].astype(f32) * value[...].astype(f32),
-        grad_out[...].astype(f32) * query[...].astype(f32),
-        filter_param[...] * filter_scale,
-    )
-    for index, part in enumerate(parts):
+    pairs = ((key_proj, k), (value, v), (grad_out, go), (query, q), (filter_param, filt))
+    copies = [pltpu.make_async_copy(source, held, sems.at[i]) for i, (source, held) in enumerate(pairs)]
+    for copy in copies:
+        copy.start()
+
+    def place(index, part):
         for piece in range(pieces):
             out[pl.ds(index * pieces + piece, channels, stride=stride), :] = part[:, piece * LANES : (piece + 1) * LANES]
+
+    copies[0].wait()
+    copies[1].wait()
+    place(0, k[...].astype(f32) * v[...].astype(f32))
+    copies[2].wait()
+    copies[3].wait()
+    place(1, go[...].astype(f32) * q[...].astype(f32))
+    copies[4].wait()
+    place(2, filt[...] * filter_scale)
 
 
 def split(values):
@@ -67,13 +75,11 @@
     return dot(left[0], right[0]) + (dot(left[0], right[1]) + dot(left[1], right[0]))
 
 
-def spectral_kernel(
-    taken, first_h, first_l, ahead_h, ahead_l, back_h, back_l, last_h, last_l, twist_cos, twist_sin, out, *, filter_scale
-):
+def spectral_kernel(taken, first_h, first_l, second_h, second_l, last_h, last_l, twists, out, *, filter_scale):
     shards = taken.shape[0]
     pieces = taken.shape[1] // 3
     half = shards * pieces
-    cos, sin = twist_cos[...], twist_sin[...]
+    cos, sin = twists[:, :LANES], twists[:, LANES:]
     stacked = jnp.concatenate(
         [taken[:, i * pieces : (i + 1) * pieces, :].reshape(half, LANES) for i in range(3)], axis=1
     )
@@ -82,22 +88,22 @@
     for i in range(3):
         real, imag = mixed[:half, i * LANES : (i + 1) * LANES], mixed[half:, i * LANES : (i + 1) * LANES]
         turned = jnp.concatenate([real * cos - imag * sin, real * sin + imag * cos], axis=1)
-        spec = product(split(turned), (ahead_h[...], ahead_l[...]))
+        spec = product(split(turned), (second_h[...], second_l[...]))
         specs.append((spec[:, :LANES], spec[:, LANES:]))
     (sig_re, sig_im), (cot_re, cot_im), (filt_re, filt_im) = specs
     results = (
-        (filt_re * sig_re - filt_im * sig_im, filt_re * sig_im + filt_im * sig_re),
-        (filt_re * cot_re + filt_im * cot_im, filt_re * cot_im - filt_im * cot_re),
+        (filt_re * sig_re - filt_im * sig_im, -(filt_re * sig_im + filt_im * sig_re)),
+        (filt_re * cot_re + filt_im * cot_im, filt_im * cot_re - filt_re * cot_im),
         (
             (cot_re * sig_re + cot_im * sig_im) * filter_scale,
-            (cot_im * sig_re - cot_re * sig_im) * filter_scale,
+            (cot_re * sig_im - cot_im * sig_re) * filter_scale,
         ),
     )
     columns = []
     for result in results:
-        spec = product(split(jnp.concatenate(result, axis=1)), (back_h[...], back_l[...]))
+        spec = product(split(jnp.concatenate(result, axis=1)), (second_h[...], second_l[...]))
         real, imag = spec[:, :LANES], spec[:, LANES:]
-        columns.append(jnp.concatenate([real * cos + imag * sin, imag * cos - real * sin], axis=0))
+        columns.append(jnp.concatenate([real * cos - imag * sin, real * sin + imag * cos], axis=0))
     timed = product((last_h[...], last_l[...]), split(jnp.concatenate(columns, axis=1)))
     for i in range(3):
         out[:, i * pieces : (i + 1) * pieces, :] = timed[:, i * LANES : (i + 1) * LANES].reshape(shards, pieces, LANES)
@@ -137,7 +143,9 @@
     gated = pl.pallas_call(
         lambda *refs: gate_kernel(*refs, filter_scale=filter_scale),
         out_shape=jax.ShapeDtypeStruct((channels * 3 * pieces, LANES), f32),
-        compiler_params=params,
+        in_specs=[pl.BlockSpec(memory_space=pltpu.HBM)] * 5,
+        scratch_shapes=[pltpu.VMEM((channels, here), jnp.bfloat16)] * 4
+        + [pltpu.VMEM((channels, here), f32), pltpu.SemaphoreType.DMA((5,))],
         name="gate",
     )(grad_out, query, key_proj, value, filter_param)
     taken = lax.all_to_all(gated.reshape(channels, 3 * pieces, LANES), "ctx", 0, 0, tiled=True)

time: 72.8 us -> 68.7 us (0.944)
  local copies, waits for them, and re-layouts: 6.13 us -> 0.08 us
  Pallas kernels: 3.69 us -> 5.53 us
    unnamed x36 -> x20, local copies, waits for them, and re-layouts: 6.12 us -> 0.07 us
    pallas_call x1, Pallas kernels: 0.07 us -> 1.91 us  [local(): pl.pallas_call(lambda *refs: gate_kernel(*refs, filter_scale=filter_scale...]
where the time goes in v1:
time: 68.7 us; the launch traced here: 68.4 us
  blocking collectives  46.4 us (68%)
  waiting for transfers between devices  8.58 us (12%)
  starting transfers between devices  7.03 us (10%)
  Pallas kernels  5.53 us (8%)
  between operations  0.77 us (1%)
    all_to_all x1, blocking collectives, local(): lax.all_to_all(gated.reshape(channels, 3 * pieces, LANES), 'ctx', 0, 0, t...  26.9 us
    all_to_all x1, blocking collectives, local(): back = lax.all_to_all(timed, 'ctx', 0, 0, tiled=True)  19.5 us
    ppermute x3, starting transfers between devices, local(): lax.ppermute(pair, 'chan', [(i, (i + 2 * step) % groups) for i in range(g...  5.92 us
    ppermute x1, waiting for transfers between devices, local(): lax.ppermute(partial, 'chan', [(i, i ^ 1) for i in range(groups)])  4.82 us
    ppermute x3, waiting for transfers between devices, local(): lax.ppermute(pair, 'chan', [(i, (i + 2 * step) % groups) for i in range(g...  3.76 us
    pallas_call x1, Pallas kernels, local(): pl.pallas_call(lambda *refs: spectral_kernel(*refs, filter_scale=filter_s...  2.15 us
    pallas_call x1, Pallas kernels, local(): pl.pallas_call(lambda *refs: gate_kernel(*refs, filter_scale=filter_scale...  1.91 us
  transfers between devices with their start and end apart: 4, of which 2 were waited for; matrix products, arithmetic and copies ran while one was open for 0% of the time, Pallas kernels for 1%

profile of v1, /device:TPU:32, one launch (start us, length us, event | category | flops | bytes accessed | tf_op | source)
XLA Modules:
  0.0 68.4 jit_solution(7721140188416556790)
XLA Ops:
  0.6 0.0 copy-start.3
  0.6 0.0 copy-start.4
  0.7 0.0 copy-start.8
  0.7 0.0 copy-start.9
  0.7 1.9 %gate.1 = f32[768,128]{1,0:T(8,128)} custom-call(bf16[32,1024]{1,0:T(8,128)(2,1)} %grad_out.1, bf16[32,1024]{1,0:T(8,128)(2,1)} %refs_1_.2, bf16[32,1024]{1,0:T(8,128)(2,1)} %key_proj.1, bf16[32,1024]{1,0:T(8,128)(2,1)} %value.1, f32[32,1024]{1,0:T(8,128)} %refs_4_.2), custom_call_target="tpu_custom_call" | custom-call | tf_op jit(solution)/shard_map/gate/pallas_call | solution.py:143
  2.6 0.0 copy-start
  2.6 0.0 copy-start.1
  2.6 0.0 copy-start.2
  2.6 26.9 %all_to_all.10.refs_0_ = f32[32,24,128]{2,1,0:T(8,128)S(1)} all-to-all(f32[32,24,128]{2,1,0:T(8,128)} %bitcast.7), channel_id=1, replica_groups=mesh['ctx'=32,'chan'=8] {'ctx'}, dimensions={0} | all-to-all | bytes 786432 | tf_op jit(solution)/shard_map/all_to_all | solution.py:151
  29.6 2.2 %spectral.1 = f32[32,24,128]{2,1,0:T(8,128)S(1)} custom-call(f32[32,24,128]{2,1,0:T(8,128)S(1)} %all_to_all.10.refs_0_, bf16[512,256]{1,0:T(8,128)(2,1)S(1)} %copy-done, bf16[512,256]{1,0:T(8,128)(2,1)S(1)} %copy-done.1, bf16[256,256]{1,0:T(8,128)(2,1)S(1)} %copy-done.8, bf16[256,256]{1,0:T(8,128)(2,1)S(1)} %copy-done.9, bf16[256,512]{1,0:T(8,128)(2,1)S(1)} %copy-done.2, ...), custom_call_target="tpu_custom_call" | custom-call | tf_op jit(solution)/shard_map/spectral/pallas_call | solution.py:153
  31.8 19.5 %all_to_all.11 = f32[32,24,128]{2,1,0:T(8,128)S(1)} all-to-all(f32[32,24,128]{2,1,0:T(8,128)S(1)} %spectral.1), channel_id=1, replica_groups=mesh['ctx'=32,'chan'=8] {'ctx'}, dimensions={0} | all-to-all | bytes 786432 | tf_op jit(solution)/shard_map/all_to_all | solution.py:159
  51.3 0.0 copy-start.5
  51.3 0.0 copy-start.6
  51.3 0.0 copy-start.7
  51.3 1.1 %collective-permute-start = (f32[256,128]{1,0:T(8,128)S(1)}, f32[256,128]{1,0:T(8,128)S(1)}, u32[]{:S(2)}, u32[]{:S(2)}) collective-permute-start(f32[256,128]{1,0:T(8,128)S(1)} %slice_bitcast_fusion), channel_id=1, source_target_pairs={{0,1},{1,0},{2,3},{3,2},{4,5},{5,4},{6,7},{7,6},{8,9},{9,8},{10,11... | collective-permute-start | bytes 393224 | tf_op jit(solution)/shard_map/ppermute | solution.py:161
  52.4 4.8 %collective-permute-done = f32[256,128]{1,0:T(8,128)S(1)} collective-permute-done((f32[256,128]{1,0:T(8,128)S(1)}, f32[256,128]{1,0:T(8,128)S(1)}, u32[]{:S(2)}, u32[]{:S(2)}) %collective-permute-start) | collective-permute-done | bytes 131104 | tf_op jit(solution)/shard_map/ppermute | solution.py:161
  57.3 1.7 %collective-permute-start.1 = (f32[256,128]{1,0:T(8,128)S(1)}, f32[256,128]{1,0:T(8,128)S(1)}, u32[]{:S(2)}, u32[]{:S(2)}) collective-permute-start(f32[256,128]{1,0:T(8,128)S(1)} %fusion.first), channel_id=1, source_target_pairs={{0,2},{1,3},{2,4},{3,5},{4,6},{5,7},{6,0},{7,1},{8,10},{9,11},{10,... | collective-permute-start | bytes 393224 | tf_op jit(solution)/shard_map/ppermute | solution.py:163
  58.9 2.9 %collective-permute-start.2 = (f32[256,128]{1,0:T(8,128)S(1)}, f32[256,128]{1,0:T(8,128)S(1)}, u32[]{:S(2)}, u32[]{:S(2)}) collective-permute-start(f32[256,128]{1,0:T(8,128)S(1)} %fusion.first), channel_id=1, source_target_pairs={{0,4},{1,5},{2,6},{3,7},{4,0},{5,1},{6,2},{7,3},{8,12},{9,13},{10,... | collective-permute-start | bytes 393224 | tf_op jit(solution)/shard_map/ppermute | solution.py:163
  61.8 1.3 %collective-permute-start.3 = (f32[256,128]{1,0:T(8,128)S(1)}, f32[256,128]{1,0:T(8,128)S(1)}, u32[]{:S(2)}, u32[]{:S(2)}) collective-permute-start(f32[256,128]{1,0:T(8,128)S(1)} %fusion.first), channel_id=1, source_target_pairs={{0,6},{1,7},{2,0},{3,1},{4,2},{5,3},{6,4},{7,5},{8,14},{9,15},{10,... | collective-permute-start | bytes 393224 | tf_op jit(solution)/shard_map/ppermute | solution.py:163
  63.2 0.7 %grads.1 = (bf16[32,1024]{1,0:T(8,128)(2,1)}, bf16[32,1024]{1,0:T(8,128)(2,1)}, bf16[32,1024]{1,0:T(8,128)(2,1)}) custom-call(f32[768,128]{1,0:T(8,128)S(1)} %bitcast.6, bf16[32,1024]{1,0:T(8,128)(2,1)S(1)} %copy-done.5, bf16[32,1024]{1,0:T(8,128)(2,1)S(1)} %copy-done.6, bf16[32,1024]{1,0:T(8,128)(2,1)S(1)} %copy-done.7), custom_call_target="tpu_custom_call" | custom-call | tf_op jit(solution)/shard_map/grads/pallas_call | solution.py:165
  63.9 0.0 collective-permute-done.1.second
  63.9 3.8 %collective-permute-done.2.third = f32[256,128]{1,0:T(8,128)S(1)} collective-permute-done((f32[256,128]{1,0:T(8,128)S(1)}, f32[256,128]{1,0:T(8,128)S(1)}, u32[]{:S(2)}, u32[]{:S(2)}) %collective-permute-start.2) | collective-permute-done | bytes 131104 | tf_op jit(solution)/shard_map/ppermute | solution.py:163
  67.7 0.0 collective-permute-done.3.fourth
  67.7 0.7 %total.1 = f32[32,1024]{1,0:T(8,128)} custom-call(f32[256,128]{1,0:T(8,128)S(1)} %fusion.first, f32[256,128]{1,0:T(8,128)S(1)} %collective-permute-done.1.second, f32[256,128]{1,0:T(8,128)S(1)} %collective-permute-done.2.third, f32[256,128]{1,0:T(8,128)S(1)} %collective-permute-done.3.fourth), custom_call_target="tpu_custom_call" | custom-call | tf_op jit(solution)/shard_map/total/pallas_call | solution.py:171
  (12 shorter events, 0.0 us)
Async XLA Ops:
  0.6 29.0 %copy-start.3 = (bf16[256,512]{1,0:T(8,128)(2,1)S(1)}, bf16[256,512]{1,0:T(8,128)(2,1)}, u32[]{:S(2)}) copy-start(bf16[256,512]{1,0:T(8,128)(2,1)} %constant.19.clone.refs_6_) | copy-start | bytes 786436
  0.6 28.9 %copy-start.4 = (f32[256,256]{1,0:T(8,128)S(1)}, f32[256,256]{1,0:T(8,128)}, u32[]{:S(2)}) copy-start(f32[256,256]{1,0:T(8,128)} %constant.20.clone.refs_7_) | copy-start | bytes 786436
  0.7 28.9 %copy-start.8 = (bf16[256,256]{1,0:T(8,128)(2,1)S(1)}, bf16[256,256]{1,0:T(8,128)(2,1)}, u32[]{:S(2)}) copy-start(bf16[256,256]{1,0:T(8,128)(2,1)} %constant.16.clone.refs_3_) | copy-start | bytes 393220
  0.7 28.9 %copy-start.9 = (bf16[256,256]{1,0:T(8,128)(2,1)S(1)}, bf16[256,256]{1,0:T(8,128)(2,1)}, u32[]{:S(2)}) copy-start(bf16[256,256]{1,0:T(8,128)(2,1)} %constant.17.clone.refs_4_) | copy-start | bytes 393220
  2.6 27.0 %copy-start = (bf16[512,256]{1,0:T(8,128)(2,1)S(1)}, bf16[512,256]{1,0:T(8,128)(2,1)}, u32[]{:S(2)}) copy-start(bf16[512,256]{1,0:T(8,128)(2,1)} %constant.14.clone.refs_1_) | copy-start | bytes 786436
  2.6 27.0 %copy-start.1 = (bf16[512,256]{1,0:T(8,128)(2,1)S(1)}, bf16[512,256]{1,0:T(8,128)(2,1)}, u32[]{:S(2)}) copy-start(bf16[512,256]{1,0:T(8,128)(2,1)} %constant.15.clone.refs_2_) | copy-start | bytes 786436
  2.6 27.0 %copy-start.2 = (bf16[256,512]{1,0:T(8,128)(2,1)S(1)}, bf16[256,512]{1,0:T(8,128)(2,1)}, u32[]{:S(2)}) copy-start(bf16[256,512]{1,0:T(8,128)(2,1)} %constant.18.clone.refs_5_) | copy-start | bytes 786436
  51.3 11.9 %copy-start.5 = (bf16[32,1024]{1,0:T(8,128)(2,1)S(1)}, bf16[32,1024]{1,0:T(8,128)(2,1)}, u32[]{:S(2)}) copy-start(bf16[32,1024]{1,0:T(8,128)(2,1)} %grad_out.1) | copy-start | bytes 196612
  51.3 11.9 %copy-start.6 = (bf16[32,1024]{1,0:T(8,128)(2,1)S(1)}, bf16[32,1024]{1,0:T(8,128)(2,1)}, u32[]{:S(2)}) copy-start(bf16[32,1024]{1,0:T(8,128)(2,1)} %key_proj.1) | copy-start | bytes 196612
  51.3 11.9 %copy-start.7 = (bf16[32,1024]{1,0:T(8,128)(2,1)S(1)}, bf16[32,1024]{1,0:T(8,128)(2,1)}, u32[]{:S(2)}) copy-start(bf16[32,1024]{1,0:T(8,128)(2,1)} %value.1) | copy-start | bytes 196612
  51.3 5.9 %collective-permute-start = (f32[256,128]{1,0:T(8,128)S(1)}, f32[256,128]{1,0:T(8,128)S(1)}, u32[]{:S(2)}, u32[]{:S(2)}) collective-permute-start(f32[256,128]{1,0:T(8,128)S(1)} %slice_bitcast_fusion), channel_id=1, source_target_pairs={{0,1},{1,0},{2,3},{3,2},{4,5},{5,4},{6,7},{7,6},{8,9},{9,8},{10,11... | collective-permute-start | bytes 393224 | tf_op jit(solution)/shard_map/ppermute | solution.py:161
  57.3 6.7 %collective-permute-start.1 = (f32[256,128]{1,0:T(8,128)S(1)}, f32[256,128]{1,0:T(8,128)S(1)}, u32[]{:S(2)}, u32[]{:S(2)}) collective-permute-start(f32[256,128]{1,0:T(8,128)S(1)} %fusion.first), channel_id=1, source_target_pairs={{0,2},{1,3},{2,4},{3,5},{4,6},{5,7},{6,0},{7,1},{8,10},{9,11},{10,... | collective-permute-start | bytes 393224 | tf_op jit(solution)/shard_map/ppermute | solution.py:163
  58.9 8.7 %collective-permute-start.2 = (f32[256,128]{1,0:T(8,128)S(1)}, f32[256,128]{1,0:T(8,128)S(1)}, u32[]{:S(2)}, u32[]{:S(2)}) collective-permute-start(f32[256,128]{1,0:T(8,128)S(1)} %fusion.first), channel_id=1, source_target_pairs={{0,4},{1,5},{2,6},{3,7},{4,0},{5,1},{6,2},{7,3},{8,12},{9,13},{10,... | collective-permute-start | bytes 393224 | tf_op jit(solution)/shard_map/ppermute | solution.py:163
  61.8 5.9 %collective-permute-start.3 = (f32[256,128]{1,0:T(8,128)S(1)}, f32[256,128]{1,0:T(8,128)S(1)}, u32[]{:S(2)}, u32[]{:S(2)}) collective-permute-start(f32[256,128]{1,0:T(8,128)S(1)} %fusion.first), channel_id=1, source_target_pairs={{0,6},{1,7},{2,0},{3,1},{4,2},{5,3},{6,4},{7,5},{8,14},{9,15},{10,... | collective-permute-start | bytes 393224 | tf_op jit(solution)/shard_map/ppermute | solution.py:163

commit v2 on v1

--- a/solution.py
+++ b/solution.py
@@ -146,8 +146,9 @@
         in_specs=[pl.BlockSpec(memory_space=pltpu.HBM)] * 5,
         scratch_shapes=[pltpu.VMEM((channels, here), jnp.bfloat16)] * 4
         + [pltpu.VMEM((channels, here), f32), pltpu.SemaphoreType.DMA((5,))],
+        compiler_params=params,
         name="gate",
-    )(grad_out, query, key_proj, value, filter_param)
+    )(*[pltpu.with_memory_space_constraint(each, pltpu.HBM) for each in (grad_out, query, key_proj, value, filter_param)])
     taken = lax.all_to_all(gated.reshape(channels, 3 * pieces, LANES), "ctx", 0, 0, tiled=True)
     tables = [jnp.asarray(table) for table in transform_tables(tokens)]
     timed = pl.pallas_call(

time: 68.7 us -> 67.7 us (0.985)
  Pallas kernels: 5.53 us -> 4.79 us
    pallas_call x1, Pallas kernels: 1.91 us -> 1.17 us  [local(): pl.pallas_call(lambda *refs: gate_kernel(*refs, filter_scale=filter_scale...]
where the time goes in v2:
time: 67.7 us; the launch traced here: 67.5 us
  blocking collectives  46.2 us (68%)
  waiting for transfers between devices  8.58 us (13%)
  starting transfers between devices  7.04 us (10%)
  Pallas kernels  4.79 us (7%)
  between operations  0.77 us (1%)
    all_to_all x1, blocking collectives, local(): lax.all_to_all(gated.reshape(channels, 3 * pieces, LANES), 'ctx', 0, 0, t...  26.7 us
    all_to_all x1, blocking collectives, local(): back = lax.all_to_all(timed, 'ctx', 0, 0, tiled=True)  19.5 us
    ppermute x3, starting transfers between devices, local(): lax.ppermute(pair, 'chan', [(i, (i + 2 * step) % groups) for i in range(g...  5.93 us
    ppermute x1, waiting for transfers between devices, local(): lax.ppermute(partial, 'chan', [(i, i ^ 1) for i in range(groups)])  4.82 us
    ppermute x3, waiting for transfers between devices, local(): lax.ppermute(pair, 'chan', [(i, (i + 2 * step) % groups) for i in range(g...  3.76 us
    pallas_call x1, Pallas kernels, local(): pl.pallas_call(lambda *refs: spectral_kernel(*refs, filter_scale=filter_s...  2.15 us
  transfers between devices with their start and end apart: 4, of which 2 were waited for; matrix products, arithmetic and copies ran while one was open for 0% of the time, Pallas kernels for 1%

profile of v2, /device:TPU:32, one launch (start us, length us, event | category | flops | bytes accessed | tf_op | source)
XLA Modules:
  0.0 67.5 jit_solution(5318662790929846224)
XLA Ops:
  0.6 0.0 copy-start.3
  0.6 0.0 copy-start.4
  0.7 0.0 copy-start.8
  0.7 0.0 copy-start.9
  0.7 1.2 %gate.1 = f32[768,128]{1,0:T(8,128)S(1)} custom-call(bf16[32,1024]{1,0:T(8,128)(2,1)} %grad_out.1, bf16[32,1024]{1,0:T(8,128)(2,1)} %refs_1_.2, bf16[32,1024]{1,0:T(8,128)(2,1)} %key_proj.1, bf16[32,1024]{1,0:T(8,128)(2,1)} %value.1, f32[32,1024]{1,0:T(8,128)} %refs_4_.2), custom_call_target="tpu_custom_call" | custom-call | tf_op jit(solution)/shard_map/gate/pallas_call | solution.py:143
  1.9 0.0 copy-start
  1.9 0.0 copy-start.1
  1.9 0.0 copy-start.2
  1.9 26.7 %all_to_all.10.refs_0_ = f32[32,24,128]{2,1,0:T(8,128)S(1)} all-to-all(f32[32,24,128]{2,1,0:T(8,128)S(1)} %bitcast.7), channel_id=1, replica_groups=mesh['ctx'=32,'chan'=8] {'ctx'}, dimensions={0} | all-to-all | bytes 786432 | tf_op jit(solution)/shard_map/all_to_all | solution.py:152
  28.7 2.2 %spectral.1 = f32[32,24,128]{2,1,0:T(8,128)S(1)} custom-call(f32[32,24,128]{2,1,0:T(8,128)S(1)} %all_to_all.10.refs_0_, bf16[512,256]{1,0:T(8,128)(2,1)S(1)} %copy-done, bf16[512,256]{1,0:T(8,128)(2,1)S(1)} %copy-done.1, bf16[256,256]{1,0:T(8,128)(2,1)S(1)} %copy-done.8, bf16[256,256]{1,0:T(8,128)(2,1)S(1)} %copy-done.9, bf16[256,512]{1,0:T(8,128)(2,1)S(1)} %copy-done.2, ...), custom_call_target="tpu_custom_call" | custom-call | tf_op jit(solution)/shard_map/spectral/pallas_call | solution.py:154
  30.8 19.5 %all_to_all.11 = f32[32,24,128]{2,1,0:T(8,128)S(1)} all-to-all(f32[32,24,128]{2,1,0:T(8,128)S(1)} %spectral.1), channel_id=1, replica_groups=mesh['ctx'=32,'chan'=8] {'ctx'}, dimensions={0} | all-to-all | bytes 786432 | tf_op jit(solution)/shard_map/all_to_all | solution.py:160
  50.3 0.0 copy-start.5
  50.3 0.0 copy-start.6
  50.3 0.0 copy-start.7
  50.4 1.1 %collective-permute-start = (f32[256,128]{1,0:T(8,128)S(1)}, f32[256,128]{1,0:T(8,128)S(1)}, u32[]{:S(2)}, u32[]{:S(2)}) collective-permute-start(f32[256,128]{1,0:T(8,128)S(1)} %slice_bitcast_fusion), channel_id=1, source_target_pairs={{0,1},{1,0},{2,3},{3,2},{4,5},{5,4},{6,7},{7,6},{8,9},{9,8},{10,11... | collective-permute-start | bytes 393224 | tf_op jit(solution)/shard_map/ppermute | solution.py:162
  51.5 4.8 %collective-permute-done = f32[256,128]{1,0:T(8,128)S(1)} collective-permute-done((f32[256,128]{1,0:T(8,128)S(1)}, f32[256,128]{1,0:T(8,128)S(1)}, u32[]{:S(2)}, u32[]{:S(2)}) %collective-permute-start) | collective-permute-done | bytes 131104 | tf_op jit(solution)/shard_map/ppermute | solution.py:162
  56.3 1.7 %collective-permute-start.1 = (f32[256,128]{1,0:T(8,128)S(1)}, f32[256,128]{1,0:T(8,128)S(1)}, u32[]{:S(2)}, u32[]{:S(2)}) collective-permute-start(f32[256,128]{1,0:T(8,128)S(1)} %fusion.first), channel_id=1, source_target_pairs={{0,2},{1,3},{2,4},{3,5},{4,6},{5,7},{6,0},{7,1},{8,10},{9,11},{10,... | collective-permute-start | bytes 393224 | tf_op jit(solution)/shard_map/ppermute | solution.py:164
  58.0 2.9 %collective-permute-start.2 = (f32[256,128]{1,0:T(8,128)S(1)}, f32[256,128]{1,0:T(8,128)S(1)}, u32[]{:S(2)}, u32[]{:S(2)}) collective-permute-start(f32[256,128]{1,0:T(8,128)S(1)} %fusion.first), channel_id=1, source_target_pairs={{0,4},{1,5},{2,6},{3,7},{4,0},{5,1},{6,2},{7,3},{8,12},{9,13},{10,... | collective-permute-start | bytes 393224 | tf_op jit(solution)/shard_map/ppermute | solution.py:164
  60.9 1.3 %collective-permute-start.3 = (f32[256,128]{1,0:T(8,128)S(1)}, f32[256,128]{1,0:T(8,128)S(1)}, u32[]{:S(2)}, u32[]{:S(2)}) collective-permute-start(f32[256,128]{1,0:T(8,128)S(1)} %fusion.first), channel_id=1, source_target_pairs={{0,6},{1,7},{2,0},{3,1},{4,2},{5,3},{6,4},{7,5},{8,14},{9,15},{10,... | collective-permute-start | bytes 393224 | tf_op jit(solution)/shard_map/ppermute | solution.py:164
  62.2 0.7 %grads.1 = (bf16[32,1024]{1,0:T(8,128)(2,1)}, bf16[32,1024]{1,0:T(8,128)(2,1)}, bf16[32,1024]{1,0:T(8,128)(2,1)}) custom-call(f32[768,128]{1,0:T(8,128)S(1)} %bitcast.6, bf16[32,1024]{1,0:T(8,128)(2,1)S(1)} %copy-done.5, bf16[32,1024]{1,0:T(8,128)(2,1)S(1)} %copy-done.6, bf16[32,1024]{1,0:T(8,128)(2,1)S(1)} %copy-done.7), custom_call_target="tpu_custom_call" | custom-call | tf_op jit(solution)/shard_map/grads/pallas_call | solution.py:166
  63.0 0.0 collective-permute-done.1.second
  63.0 3.8 %collective-permute-done.2.third = f32[256,128]{1,0:T(8,128)S(1)} collective-permute-done((f32[256,128]{1,0:T(8,128)S(1)}, f32[256,128]{1,0:T(8,128)S(1)}, u32[]{:S(2)}, u32[]{:S(2)}) %collective-permute-start.2) | collective-permute-done | bytes 131104 | tf_op jit(solution)/shard_map/ppermute | solution.py:164
  66.7 0.0 collective-permute-done.3.fourth
  66.7 0.7 %total.1 = f32[32,1024]{1,0:T(8,128)} custom-call(f32[256,128]{1,0:T(8,128)S(1)} %fusion.first, f32[256,128]{1,0:T(8,128)S(1)} %collective-permute-done.1.second, f32[256,128]{1,0:T(8,128)S(1)} %collective-permute-done.2.third, f32[256,128]{1,0:T(8,128)S(1)} %collective-permute-done.3.fourth), custom_call_target="tpu_custom_call" | custom-call | tf_op jit(solution)/shard_map/total/pallas_call | solution.py:172
  (12 shorter events, 0.0 us)
Async XLA Ops:
  0.6 28.0 %copy-start.3 = (bf16[256,512]{1,0:T(8,128)(2,1)S(1)}, bf16[256,512]{1,0:T(8,128)(2,1)}, u32[]{:S(2)}) copy-start(bf16[256,512]{1,0:T(8,128)(2,1)} %constant.19.clone.refs_6_) | copy-start | bytes 786436
  0.6 28.0 %copy-start.4 = (f32[256,256]{1,0:T(8,128)S(1)}, f32[256,256]{1,0:T(8,128)}, u32[]{:S(2)}) copy-start(f32[256,256]{1,0:T(8,128)} %constant.20.clone.refs_7_) | copy-start | bytes 786436
  0.7 28.0 %copy-start.8 = (bf16[256,256]{1,0:T(8,128)(2,1)S(1)}, bf16[256,256]{1,0:T(8,128)(2,1)}, u32[]{:S(2)}) copy-start(bf16[256,256]{1,0:T(8,128)(2,1)} %constant.16.clone.refs_3_) | copy-start | bytes 393220
  0.7 28.0 %copy-start.9 = (bf16[256,256]{1,0:T(8,128)(2,1)S(1)}, bf16[256,256]{1,0:T(8,128)(2,1)}, u32[]{:S(2)}) copy-start(bf16[256,256]{1,0:T(8,128)(2,1)} %constant.17.clone.refs_4_) | copy-start | bytes 393220
  1.9 26.8 %copy-start = (bf16[512,256]{1,0:T(8,128)(2,1)S(1)}, bf16[512,256]{1,0:T(8,128)(2,1)}, u32[]{:S(2)}) copy-start(bf16[512,256]{1,0:T(8,128)(2,1)} %constant.14.clone.refs_1_) | copy-start | bytes 786436
  1.9 26.8 %copy-start.1 = (bf16[512,256]{1,0:T(8,128)(2,1)S(1)}, bf16[512,256]{1,0:T(8,128)(2,1)}, u32[]{:S(2)}) copy-start(bf16[512,256]{1,0:T(8,128)(2,1)} %constant.15.clone.refs_2_) | copy-start | bytes 786436
  1.9 26.8 %copy-start.2 = (bf16[256,512]{1,0:T(8,128)(2,1)S(1)}, bf16[256,512]{1,0:T(8,128)(2,1)}, u32[]{:S(2)}) copy-start(bf16[256,512]{1,0:T(8,128)(2,1)} %constant.18.clone.refs_5_) | copy-start | bytes 786436
  50.3 11.9 %copy-start.5 = (bf16[32,1024]{1,0:T(8,128)(2,1)S(1)}, bf16[32,1024]{1,0:T(8,128)(2,1)}, u32[]{:S(2)}) copy-start(bf16[32,1024]{1,0:T(8,128)(2,1)} %grad_out.1) | copy-start | bytes 196612
  50.3 11.9 %copy-start.6 = (bf16[32,1024]{1,0:T(8,128)(2,1)S(1)}, bf16[32,1024]{1,0:T(8,128)(2,1)}, u32[]{:S(2)}) copy-start(bf16[32,1024]{1,0:T(8,128)(2,1)} %key_proj.1) | copy-start | bytes 196612
  50.3 11.9 %copy-start.7 = (bf16[32,1024]{1,0:T(8,128)(2,1)S(1)}, bf16[32,1024]{1,0:T(8,128)(2,1)}, u32[]{:S(2)}) copy-start(bf16[32,1024]{1,0:T(8,128)(2,1)} %value.1) | copy-start | bytes 196612
  50.4 5.9 %collective-permute-start = (f32[256,128]{1,0:T(8,128)S(1)}, f32[256,128]{1,0:T(8,128)S(1)}, u32[]{:S(2)}, u32[]{:S(2)}) collective-permute-start(f32[256,128]{1,0:T(8,128)S(1)} %slice_bitcast_fusion), channel_id=1, source_target_pairs={{0,1},{1,0},{2,3},{3,2},{4,5},{5,4},{6,7},{7,6},{8,9},{9,8},{10,11... | collective-permute-start | bytes 393224 | tf_op jit(solution)/shard_map/ppermute | solution.py:162
  56.3 6.7 %collective-permute-start.1 = (f32[256,128]{1,0:T(8,128)S(1)}, f32[256,128]{1,0:T(8,128)S(1)}, u32[]{:S(2)}, u32[]{:S(2)}) collective-permute-start(f32[256,128]{1,0:T(8,128)S(1)} %fusion.first), channel_id=1, source_target_pairs={{0,2},{1,3},{2,4},{3,5},{4,6},{5,7},{6,0},{7,1},{8,10},{9,11},{10,... | collective-permute-start | bytes 393224 | tf_op jit(solution)/shard_map/ppermute | solution.py:164
  58.0 8.8 %collective-permute-start.2 = (f32[256,128]{1,0:T(8,128)S(1)}, f32[256,128]{1,0:T(8,128)S(1)}, u32[]{:S(2)}, u32[]{:S(2)}) collective-permute-start(f32[256,128]{1,0:T(8,128)S(1)} %fusion.first), channel_id=1, source_target_pairs={{0,4},{1,5},{2,6},{3,7},{4,0},{5,1},{6,2},{7,3},{8,12},{9,13},{10,... | collective-permute-start | bytes 393224 | tf_op jit(solution)/shard_map/ppermute | solution.py:164
  60.9 5.9 %collective-permute-start.3 = (f32[256,128]{1,0:T(8,128)S(1)}, f32[256,128]{1,0:T(8,128)S(1)}, u32[]{:S(2)}, u32[]{:S(2)}) collective-permute-start(f32[256,128]{1,0:T(8,128)S(1)} %fusion.first), channel_id=1, source_target_pairs={{0,6},{1,7},{2,0},{3,1},{4,2},{5,3},{6,4},{7,5},{8,14},{9,15},{10,... | collective-permute-start | bytes 393224 | tf_op jit(solution)/shard_map/ppermute | solution.py:164

commit v3 on v2

--- a/solution.py
+++ b/solution.py
@@ -68,11 +68,25 @@
     return high, low
 
 
-def product(left, right):
-    def dot(a, b):
-        return jnp.dot(a, b, preferred_element_type=jnp.float32)
+def dot(left, right):
+    return jnp.dot(left, right, preferred_element_type=jnp.float32)
 
-    return dot(left[0], right[0]) + (dot(left[0], right[1]) + dot(left[1], right[0]))
+
+def times_table(values, table):
+    high, low = split(values)
+    table_high, table_low = table
+    return dot(high, table_high) + (dot(high, table_low) + dot(low, table_high))
+
+
+def table_times(table, columns):
+    table_high, table_low = table
+    parts = [split(column) for column in columns]
+    lows = dot(table_low, jnp.concatenate([high for high, _ in parts], axis=1))
+    results = []
+    for i, part in enumerate(parts):
+        both = dot(table_high, jnp.concatenate(part, axis=1))
+        results.append(both[:, :LANES] + (both[:, LANES:] + lows[:, i * LANES : (i + 1) * LANES]))
+    return results
 
 
 def spectral_kernel(taken, first_h, first_l, second_h, second_l, last_h, last_l, twists, out, *, filter_scale):
@@ -80,15 +94,15 @@
     pieces = taken.shape[1] // 3
     half = shards * pieces
     cos, sin = twists[:, :LANES], twists[:, LANES:]
-    stacked = jnp.concatenate(
-        [taken[:, i * pieces : (i + 1) * pieces, :].reshape(half, LANES) for i in range(3)], axis=1
-    )
-    mixed = product((first_h[...], first_l[...]), split(stacked))
+    first, second, last = (first_h[...], first_l[...]), (second_h[...], second_l[...]), (last_h[...], last_l[...])
+
+    def turn(real, imag):
+        return real * cos - imag * sin, real * sin + imag * cos
+
+    mixed = table_times(first, [taken[:, i * pieces : (i + 1) * pieces, :].reshape(half, LANES) for i in range(3)])
     specs = []
-    for i in range(3):
-        real, imag = mixed[:half, i * LANES : (i + 1) * LANES], mixed[half:, i * LANES : (i + 1) * LANES]
-        turned = jnp.concatenate([real * cos - imag * sin, real * sin + imag * cos], axis=1)
-        spec = product(split(turned), (second_h[...], second_l[...]))
+    for each in mixed:
+        spec = times_table(jnp.concatenate(turn(each[:half], each[half:]), axis=1), second)
         specs.append((spec[:, :LANES], spec[:, LANES:]))
     (sig_re, sig_im), (cot_re, cot_im), (filt_re, filt_im) = specs
     results = (
@@ -99,14 +113,13 @@
             (cot_re * sig_im - cot_im * sig_re) * filter_scale,
         ),
     )
+    order = (2, 0, 1)
     columns = []
-    for result in results:
-        spec = product(split(jnp.concatenate(result, axis=1)), (second_h[...], second_l[...]))
-        real, imag = spec[:, :LANES], spec[:, LANES:]
-        columns.append(jnp.concatenate([real * cos - imag * sin, real * sin + imag * cos], axis=0))
-    timed = product((last_h[...], last_l[...]), split(jnp.concatenate(columns, axis=1)))
-    for i in range(3):
-        out[:, i * pieces : (i + 1) * pieces, :] = timed[:, i * LANES : (i + 1) * LANES].reshape(shards, pieces, LANES)
+    for i in order:
+        spec = times_table(jnp.concatenate(results[i], axis=1), second)
+        columns.append(jnp.concatenate(turn(spec[:, :LANES], spec[:, LANES:]), axis=0))
+    for i, timed in zip(order, table_times(last, columns)):
+        out[:, i * pieces : (i + 1) * pieces, :] = timed.reshape(shards, pieces, LANES)
 
 
 def grads_kernel(back, grad_out, key_proj, value, grad_query, grad_key, grad_value):

time: 67.7 us -> 67.2 us (level)
  no operation moved by 1% of the time
where the time goes in v3:
time: 67.2 us; the launch traced here: 67 us
  blocking collectives  46.2 us (69%)
  waiting for transfers between devices  8.56 us (13%)
  starting transfers between devices  7.01 us (10%)
  Pallas kernels  4.39 us (7%)
  between operations  0.77 us (1%)
    all_to_all x1, blocking collectives, local(): lax.all_to_all(gated.reshape(channels, 3 * pieces, LANES), 'ctx', 0, 0, t...  26.7 us
    all_to_all x1, blocking collectives, local(): back = lax.all_to_all(timed, 'ctx', 0, 0, tiled=True)  19.5 us
    ppermute x3, starting transfers between devices, local(): lax.ppermute(pair, 'chan', [(i, (i + 2 * step) % groups) for i in range(g...  5.9 us
    ppermute x1, waiting for transfers between devices, local(): lax.ppermute(partial, 'chan', [(i, i ^ 1) for i in range(groups)])  4.82 us
    ppermute x3, waiting for transfers between devices, local(): lax.ppermute(pair, 'chan', [(i, (i + 2 * step) % groups) for i in range(g...  3.74 us
    pallas_call x1, Pallas kernels, local(): pl.pallas_call(lambda *refs: spectral_kernel(*refs, filter_scale=filter_s...  1.75 us
  transfers between devices with their start and end apart: 4, of which 2 were waited for; matrix products, arithmetic and copies ran while one was open for 0% of the time, Pallas kernels for 1%

profile of v3, /device:TPU:32, one launch (start us, length us, event | category | flops | bytes accessed | tf_op | source)
XLA Modules:
  0.0 67.0 jit_solution(1305682804075253742)
XLA Ops:
  0.6 0.0 copy-start.3
  0.6 0.0 copy-start.4
  0.7 0.0 copy-start.8
  0.7 0.0 copy-start.9
  0.7 1.2 %gate.1 = f32[768,128]{1,0:T(8,128)S(1)} custom-call(bf16[32,1024]{1,0:T(8,128)(2,1)} %grad_out.1, bf16[32,1024]{1,0:T(8,128)(2,1)} %refs_1_.2, bf16[32,1024]{1,0:T(8,128)(2,1)} %key_proj.1, bf16[32,1024]{1,0:T(8,128)(2,1)} %value.1, f32[32,1024]{1,0:T(8,128)} %refs_4_.2), custom_call_target="tpu_custom_call" | custom-call | tf_op jit(solution)/shard_map/gate/pallas_call | solution.py:156
  1.9 0.0 copy-start
  1.9 0.0 copy-start.1
  1.9 0.0 copy-start.2
  1.9 26.7 %all_to_all.10.refs_0_ = f32[32,24,128]{2,1,0:T(8,128)S(1)} all-to-all(f32[32,24,128]{2,1,0:T(8,128)S(1)} %bitcast.7), channel_id=1, replica_groups=mesh['ctx'=32,'chan'=8] {'ctx'}, dimensions={0} | all-to-all | bytes 786432 | tf_op jit(solution)/shard_map/all_to_all | solution.py:165
  28.7 1.8 %spectral.1 = f32[32,24,128]{2,1,0:T(8,128)S(1)} custom-call(f32[32,24,128]{2,1,0:T(8,128)S(1)} %all_to_all.10.refs_0_, bf16[512,256]{1,0:T(8,128)(2,1)S(1)} %copy-done, bf16[512,256]{1,0:T(8,128)(2,1)S(1)} %copy-done.1, bf16[256,256]{1,0:T(8,128)(2,1)S(1)} %copy-done.8, bf16[256,256]{1,0:T(8,128)(2,1)S(1)} %copy-done.9, bf16[256,512]{1,0:T(8,128)(2,1)S(1)} %copy-done.2, ...), custom_call_target="tpu_custom_call" | custom-call | tf_op jit(solution)/shard_map/spectral/pallas_call | solution.py:167
  30.4 19.5 %all_to_all.11 = f32[32,24,128]{2,1,0:T(8,128)S(1)} all-to-all(f32[32,24,128]{2,1,0:T(8,128)S(1)} %spectral.1), channel_id=1, replica_groups=mesh['ctx'=32,'chan'=8] {'ctx'}, dimensions={0} | all-to-all | bytes 786432 | tf_op jit(solution)/shard_map/all_to_all | solution.py:173
  49.9 0.0 copy-start.5
  49.9 0.0 copy-start.6
  49.9 0.0 copy-start.7
  50.0 1.1 %collective-permute-start = (f32[256,128]{1,0:T(8,128)S(1)}, f32[256,128]{1,0:T(8,128)S(1)}, u32[]{:S(2)}, u32[]{:S(2)}) collective-permute-start(f32[256,128]{1,0:T(8,128)S(1)} %slice_bitcast_fusion), channel_id=1, source_target_pairs={{0,1},{1,0},{2,3},{3,2},{4,5},{5,4},{6,7},{7,6},{8,9},{9,8},{10,11... | collective-permute-start | bytes 393224 | tf_op jit(solution)/shard_map/ppermute | solution.py:175
  51.1 4.8 %collective-permute-done = f32[256,128]{1,0:T(8,128)S(1)} collective-permute-done((f32[256,128]{1,0:T(8,128)S(1)}, f32[256,128]{1,0:T(8,128)S(1)}, u32[]{:S(2)}, u32[]{:S(2)}) %collective-permute-start) | collective-permute-done | bytes 131104 | tf_op jit(solution)/shard_map/ppermute | solution.py:175
  55.9 1.7 %collective-permute-start.1 = (f32[256,128]{1,0:T(8,128)S(1)}, f32[256,128]{1,0:T(8,128)S(1)}, u32[]{:S(2)}, u32[]{:S(2)}) collective-permute-start(f32[256,128]{1,0:T(8,128)S(1)} %fusion.first), channel_id=1, source_target_pairs={{0,2},{1,3},{2,4},{3,5},{4,6},{5,7},{6,0},{7,1},{8,10},{9,11},{10,... | collective-permute-start | bytes 393224 | tf_op jit(solution)/shard_map/ppermute | solution.py:177
  57.6 2.9 %collective-permute-start.2 = (f32[256,128]{1,0:T(8,128)S(1)}, f32[256,128]{1,0:T(8,128)S(1)}, u32[]{:S(2)}, u32[]{:S(2)}) collective-permute-start(f32[256,128]{1,0:T(8,128)S(1)} %fusion.first), channel_id=1, source_target_pairs={{0,4},{1,5},{2,6},{3,7},{4,0},{5,1},{6,2},{7,3},{8,12},{9,13},{10,... | collective-permute-start | bytes 393224 | tf_op jit(solution)/shard_map/ppermute | solution.py:177
  60.5 1.3 %collective-permute-start.3 = (f32[256,128]{1,0:T(8,128)S(1)}, f32[256,128]{1,0:T(8,128)S(1)}, u32[]{:S(2)}, u32[]{:S(2)}) collective-permute-start(f32[256,128]{1,0:T(8,128)S(1)} %fusion.first), channel_id=1, source_target_pairs={{0,6},{1,7},{2,0},{3,1},{4,2},{5,3},{6,4},{7,5},{8,14},{9,15},{10,... | collective-permute-start | bytes 393224 | tf_op jit(solution)/shard_map/ppermute | solution.py:177
  61.8 0.7 %grads.1 = (bf16[32,1024]{1,0:T(8,128)(2,1)}, bf16[32,1024]{1,0:T(8,128)(2,1)}, bf16[32,1024]{1,0:T(8,128)(2,1)}) custom-call(f32[768,128]{1,0:T(8,128)S(1)} %bitcast.6, bf16[32,1024]{1,0:T(8,128)(2,1)S(1)} %copy-done.5, bf16[32,1024]{1,0:T(8,128)(2,1)S(1)} %copy-done.6, bf16[32,1024]{1,0:T(8,128)(2,1)S(1)} %copy-done.7), custom_call_target="tpu_custom_call" | custom-call | tf_op jit(solution)/shard_map/grads/pallas_call | solution.py:179
  62.5 0.0 collective-permute-done.1.second
  62.6 3.7 %collective-permute-done.2.third = f32[256,128]{1,0:T(8,128)S(1)} collective-permute-done((f32[256,128]{1,0:T(8,128)S(1)}, f32[256,128]{1,0:T(8,128)S(1)}, u32[]{:S(2)}, u32[]{:S(2)}) %collective-permute-start.2) | collective-permute-done | bytes 131104 | tf_op jit(solution)/shard_map/ppermute | solution.py:177
  66.3 0.0 collective-permute-done.3.fourth
  66.3 0.7 %total.1 = f32[32,1024]{1,0:T(8,128)} custom-call(f32[256,128]{1,0:T(8,128)S(1)} %fusion.first, f32[256,128]{1,0:T(8,128)S(1)} %collective-permute-done.1.second, f32[256,128]{1,0:T(8,128)S(1)} %collective-permute-done.2.third, f32[256,128]{1,0:T(8,128)S(1)} %collective-permute-done.3.fourth), custom_call_target="tpu_custom_call" | custom-call | tf_op jit(solution)/shard_map/total/pallas_call | solution.py:185
  (12 shorter events, 0.0 us)
Async XLA Ops:
  0.6 28.0 %copy-start.3 = (bf16[256,512]{1,0:T(8,128)(2,1)S(1)}, bf16[256,512]{1,0:T(8,128)(2,1)}, u32[]{:S(2)}) copy-start(bf16[256,512]{1,0:T(8,128)(2,1)} %constant.19.clone.refs_6_) | copy-start | bytes 786436
  0.6 28.0 %copy-start.4 = (f32[256,256]{1,0:T(8,128)S(1)}, f32[256,256]{1,0:T(8,128)}, u32[]{:S(2)}) copy-start(f32[256,256]{1,0:T(8,128)} %constant.20.clone.refs_7_) | copy-start | bytes 786436
  0.7 28.0 %copy-start.8 = (bf16[256,256]{1,0:T(8,128)(2,1)S(1)}, bf16[256,256]{1,0:T(8,128)(2,1)}, u32[]{:S(2)}) copy-start(bf16[256,256]{1,0:T(8,128)(2,1)} %constant.16.clone.refs_3_) | copy-start | bytes 393220
  0.7 28.0 %copy-start.9 = (bf16[256,256]{1,0:T(8,128)(2,1)S(1)}, bf16[256,256]{1,0:T(8,128)(2,1)}, u32[]{:S(2)}) copy-start(bf16[256,256]{1,0:T(8,128)(2,1)} %constant.17.clone.refs_4_) | copy-start | bytes 393220
  1.9 26.8 %copy-start = (bf16[512,256]{1,0:T(8,128)(2,1)S(1)}, bf16[512,256]{1,0:T(8,128)(2,1)}, u32[]{:S(2)}) copy-start(bf16[512,256]{1,0:T(8,128)(2,1)} %constant.14.clone.refs_1_) | copy-start | bytes 786436
  1.9 26.8 %copy-start.1 = (bf16[512,256]{1,0:T(8,128)(2,1)S(1)}, bf16[512,256]{1,0:T(8,128)(2,1)}, u32[]{:S(2)}) copy-start(bf16[512,256]{1,0:T(8,128)(2,1)} %constant.15.clone.refs_2_) | copy-start | bytes 786436
  1.9 26.8 %copy-start.2 = (bf16[256,512]{1,0:T(8,128)(2,1)S(1)}, bf16[256,512]{1,0:T(8,128)(2,1)}, u32[]{:S(2)}) copy-start(bf16[256,512]{1,0:T(8,128)(2,1)} %constant.18.clone.refs_5_) | copy-start | bytes 786436
  49.9 11.9 %copy-start.5 = (bf16[32,1024]{1,0:T(8,128)(2,1)S(1)}, bf16[32,1024]{1,0:T(8,128)(2,1)}, u32[]{:S(2)}) copy-start(bf16[32,1024]{1,0:T(8,128)(2,1)} %grad_out.1) | copy-start | bytes 196612
  49.9 11.9 %copy-start.6 = (bf16[32,1024]{1,0:T(8,128)(2,1)S(1)}, bf16[32,1024]{1,0:T(8,128)(2,1)}, u32[]{:S(2)}) copy-start(bf16[32,1024]{1,0:T(8,128)(2,1)} %key_proj.1) | copy-start | bytes 196612
  49.9 11.9 %copy-start.7 = (bf16[32,1024]{1,0:T(8,128)(2,1)S(1)}, bf16[32,1024]{1,0:T(8,128)(2,1)}, u32[]{:S(2)}) copy-start(bf16[32,1024]{1,0:T(8,128)(2,1)} %value.1) | copy-start | bytes 196612
  50.0 5.9 %collective-permute-start = (f32[256,128]{1,0:T(8,128)S(1)}, f32[256,128]{1,0:T(8,128)S(1)}, u32[]{:S(2)}, u32[]{:S(2)}) collective-permute-start(f32[256,128]{1,0:T(8,128)S(1)} %slice_bitcast_fusion), channel_id=1, source_target_pairs={{0,1},{1,0},{2,3},{3,2},{4,5},{5,4},{6,7},{7,6},{8,9},{9,8},{10,11... | collective-permute-start | bytes 393224 | tf_op jit(solution)/shard_map/ppermute | solution.py:175
  55.9 6.7 %collective-permute-start.1 = (f32[256,128]{1,0:T(8,128)S(1)}, f32[256,128]{1,0:T(8,128)S(1)}, u32[]{:S(2)}, u32[]{:S(2)}) collective-permute-start(f32[256,128]{1,0:T(8,128)S(1)} %fusion.first), channel_id=1, source_target_pairs={{0,2},{1,3},{2,4},{3,5},{4,6},{5,7},{6,0},{7,1},{8,10},{9,11},{10,... | collective-permute-start | bytes 393224 | tf_op jit(solution)/shard_map/ppermute | solution.py:177
  57.6 8.7 %collective-permute-start.2 = (f32[256,128]{1,0:T(8,128)S(1)}, f32[256,128]{1,0:T(8,128)S(1)}, u32[]{:S(2)}, u32[]{:S(2)}) collective-permute-start(f32[256,128]{1,0:T(8,128)S(1)} %fusion.first), channel_id=1, source_target_pairs={{0,4},{1,5},{2,6},{3,7},{4,0},{5,1},{6,2},{7,3},{8,12},{9,13},{10,... | collective-permute-start | bytes 393224 | tf_op jit(solution)/shard_map/ppermute | solution.py:177
  60.5 5.8 %collective-permute-start.3 = (f32[256,128]{1,0:T(8,128)S(1)}, f32[256,128]{1,0:T(8,128)S(1)}, u32[]{:S(2)}, u32[]{:S(2)}) collective-permute-start(f32[256,128]{1,0:T(8,128)S(1)} %fusion.first), channel_id=1, source_target_pairs={{0,6},{1,7},{2,0},{3,1},{4,2},{5,3},{6,4},{7,5},{8,14},{9,15},{10,... | collective-permute-start | bytes 393224 | tf_op jit(solution)/shard_map/ppermute | solution.py:177

commit v4 on v3

--- a/solution.py
+++ b/solution.py
@@ -89,59 +89,66 @@
     return results
 
 
-def spectral_kernel(taken, first_h, first_l, second_h, second_l, last_h, last_l, twists, out, *, filter_scale):
-    shards = taken.shape[0]
-    pieces = taken.shape[1] // 3
+def turn(real, imag, twists):
+    cos, sin = twists[:, :LANES], twists[:, LANES:]
+    return jnp.concatenate([real * cos - imag * sin, real * sin + imag * cos], axis=1)
+
+
+def forward(columns, first, second, twists):
+    half = columns[0].shape[0]
+    specs = [times_table(turn(mixed[:half], mixed[half:], twists), second) for mixed in table_times(first, columns)]
+    return [(spec[:, :LANES], spec[:, LANES:]) for spec in specs]
+
+
+def backward(spectra, second, last, twists):
+    columns = []
+    for spectrum in spectra:
+        spec = times_table(jnp.concatenate(spectrum, axis=1), second)
+        turned = turn(spec[:, :LANES], spec[:, LANES:], twists)
+        columns.append(jnp.concatenate([turned[:, :LANES], turned[:, LANES:]], axis=0))
+    return table_times(last, columns)
+
+
+def spectral_kernel(
+    taken, first_h, first_l, second_h, second_l, last_h, last_l, twists, timed, corr, held, sem, *, filter_scale
+):
+    shards, pieces, _ = corr.shape
     half = shards * pieces
-    cos, sin = twists[:, :LANES], twists[:, LANES:]
     first, second, last = (first_h[...], first_l[...]), (second_h[...], second_l[...]), (last_h[...], last_l[...])
-
-    def turn(real, imag):
-        return real * cos - imag * sin, real * sin + imag * cos
-
-    mixed = table_times(first, [taken[:, i * pieces : (i + 1) * pieces, :].reshape(half, LANES) for i in range(3)])
-    specs = []
-    for each in mixed:
-        spec = times_table(jnp.concatenate(turn(each[:half], each[half:]), axis=1), second)
-        specs.append((spec[:, :LANES], spec[:, LANES:]))
-    (sig_re, sig_im), (cot_re, cot_im), (filt_re, filt_im) = specs
-    results = (
+    columns = [taken[:, i * pieces : (i + 1) * pieces, :].reshape(half, LANES) for i in range(3)]
+    (sig_re, sig_im), (cot_re, cot_im), (filt_re, filt_im) = forward(columns, first, second, twists[...])
+    spectra = [
         (filt_re * sig_re - filt_im * sig_im, -(filt_re * sig_im + filt_im * sig_re)),
         (filt_re * cot_re + filt_im * cot_im, filt_im * cot_re - filt_re * cot_im),
-        (
-            (cot_re * sig_re + cot_im * sig_im) * filter_scale,
-            (cot_re * sig_im - cot_im * sig_re) * filter_scale,
-        ),
+    ]
+    for i, part in enumerate(backward(spectra, second, last, twists[...])):
+        held[:, i * pieces : (i + 1) * pieces, :] = part.reshape(shards, pieces, LANES)
+    copy = pltpu.make_async_copy(held, timed, sem)
+    copy.start()
+    spectrum = (
+        (cot_re * sig_re + cot_im * sig_im) * filter_scale,
+        (cot_re * sig_im - cot_im * sig_re) * filter_scale,
     )
-    order = (2, 0, 1)
-    columns = []
-    for i in order:
-        spec = times_table(jnp.concatenate(results[i], axis=1), second)
-        columns.append(jnp.concatenate(turn(spec[:, :LANES], spec[:, LANES:]), axis=0))
-    for i, timed in zip(order, table_times(last, columns)):
-        out[:, i * pieces : (i + 1) * pieces, :] = timed.reshape(shards, pieces, LANES)
-
-
-def grads_kernel(back, grad_out, key_proj, value, grad_query, grad_key, grad_value):
+    (part,) = backward([spectrum], second, last, twists[...])
+    corr[...] = part.reshape(shards, pieces, LANES)
+    copy.wait()
+
+
+def grads_kernel(
+    back, grad_out, key_proj, value, total, swapped, grad_query, grad_key, grad_value, grad_filter
+):
     f32 = jnp.float32
     channels, here = key_proj.shape
     pieces = here // LANES
-    stride = 3 * pieces
     for piece in range(pieces):
         columns = slice(piece * LANES, (piece + 1) * LANES)
-        conv = back[pl.ds(piece, channels, stride=stride), :]
-        grad_signal = back[pl.ds(pieces + piece, channels, stride=stride), :]
+        rows = pl.ds(piece, channels, stride=pieces)
+        grad_filter[:, columns] = total[rows, :] + swapped[rows, :]
+        conv = back[pl.ds(piece, channels, stride=2 * pieces), :]
+        grad_signal = back[pl.ds(pieces + piece, channels, stride=2 * pieces), :]
         grad_query[:, columns] = (grad_out[:, columns].astype(f32) * conv).astype(jnp.bfloat16)
         grad_key[:, columns] = (grad_signal * value[:, columns].astype(f32)).astype(jnp.bfloat16)
         grad_value[:, columns] = (grad_signal * key_proj[:, columns].astype(f32)).astype(jnp.bfloat16)
-
-
-def total_kernel(first, second, third, fourth, out):
-    channels, here = out.shape
-    pieces = here // LANES
-    for piece in range(pieces):
-        rows = pl.ds(piece, channels, stride=pieces)
-        out[:, piece * LANES : (piece + 1) * LANES] = (first[rows, :] + second[rows, :]) + (third[rows, :] + fourth[rows, :])
 
 
 def local(grad_out, query, key_proj, value, filter_param):
@@ -164,30 +171,29 @@
     )(*[pltpu.with_memory_space_constraint(each, pltpu.HBM) for each in (grad_out, query, key_proj, value, filter_param)])
     taken = lax.all_to_all(gated.reshape(channels, 3 * pieces, LANES), "ctx", 0, 0, tiled=True)
     tables = [jnp.asarray(table) for table in transform_tables(tokens)]
-    timed = pl.pallas_call(
+    timed, corr = pl.pallas_call(
         lambda *refs: spectral_kernel(*refs, filter_scale=filter_scale),
-        out_shape=jax.ShapeDtypeStruct((shards, 3 * pieces, LANES), f32),
+        out_shape=[
+            jax.ShapeDtypeStruct((shards, 2 * pieces, LANES), f32),
+            jax.ShapeDtypeStruct((shards, pieces, LANES), f32),
+        ],
+        out_specs=[pl.BlockSpec(memory_space=pltpu.HBM), pl.BlockSpec(memory_space=pltpu.VMEM)],
+        scratch_shapes=[pltpu.VMEM((shards, 2 * pieces, LANES), f32), pltpu.SemaphoreType.DMA(())],
         compiler_params=params,
         name="spectral",
     )(taken, *tables)
+    partial = lax.all_to_all(corr, "ctx", 0, 0, tiled=True).reshape(channels * pieces, LANES)
     back = lax.all_to_all(timed, "ctx", 0, 0, tiled=True)
-    partial = back[:, 2 * pieces :, :].reshape(channels * pieces, LANES)
-    pair = partial + lax.ppermute(partial, "chan", [(i, i ^ 1) for i in range(groups)])
-    others = [
-        lax.ppermute(pair, "chan", [(i, (i + 2 * step) % groups) for i in range(groups)]) for step in range(1, groups // 2)
-    ]
-    grad_query, grad_key, grad_value = pl.pallas_call(
+    total = partial + lax.ppermute(partial, "chan", [(i, i ^ 2) for i in range(groups)])
+    total = total + lax.ppermute(total, "chan", [(i, 2 * (groups // 2 - 1 - i // 2) + i % 2) for i in range(groups)])
+    swapped = lax.ppermute(total, "chan", [(i, i ^ 1) for i in range(groups)])
+    grad_query, grad_key, grad_value, grad_filter = pl.pallas_call(
         grads_kernel,
-        out_shape=[jax.ShapeDtypeStruct((channels, here), jnp.bfloat16)] * 3,
+        out_shape=[jax.ShapeDtypeStruct((channels, here), jnp.bfloat16)] * 3
+        + [jax.ShapeDtypeStruct((channels, here), f32)],
         compiler_params=params,
         name="grads",
-    )(back.reshape(channels * 3 * pieces, LANES), grad_out, key_proj, value)
-    grad_filter = pl.pallas_call(
-        total_kernel,
-        out_shape=jax.ShapeDtypeStruct((channels, here), f32),
-        compiler_params=params,
-        name="total",
-    )(pair, *others)
+    )(back.reshape(channels * 2 * pieces, LANES), grad_out, key_proj, value, total, swapped)
     return (grad_query, grad_key, grad_value, grad_filter)
 
 

time: 67.2 us -> 66.9 us (level)
  the two profiles are of different devices: /device:TPU:32 before, /device:TPU:1 now
where the time goes in v4:
time: 66.9 us; the launch traced here: 66.7 us
  blocking collectives  43 us (64%)
  waiting for transfers between devices  9.47 us (14%)
  starting transfers between devices  8.9 us (13%)
  Pallas kernels  4.41 us (7%)
  between operations  0.8 us (1%)
    all_to_all x1, blocking collectives, local(): lax.all_to_all(gated.reshape(channels, 3 * pieces, LANES), 'ctx', 0, 0, t...  27.9 us
    all_to_all x1, blocking collectives, local(): lax.all_to_all(corr, 'ctx', 0, 0, tiled=True)  15.1 us
    all_to_all x1, waiting for transfers between devices, local(): back = lax.all_to_all(timed, 'ctx', 0, 0, tiled=True)  6.26 us
    all_to_all x1, starting transfers between devices, local(): back = lax.all_to_all(timed, 'ctx', 0, 0, tiled=True)  3.96 us
    ppermute x1, waiting for transfers between devices, local(): lax.ppermute(total, 'chan', [(i, 2 * (groups // 2 - 1 - i // 2) + i % 2)...  3.21 us
    ppermute x1, starting transfers between devices, local(): lax.ppermute(total, 'chan', [(i, 2 * (groups // 2 - 1 - i // 2) + i % 2)...  2.49 us
    pallas_call x1, Pallas kernels, local(): pl.pallas_call(lambda *refs: spectral_kernel(*refs, filter_scale=filter_s...  2.38 us
  transfers between devices with their start and end apart: 4, of which 2 were waited for; matrix products, arithmetic and copies ran while one was open for 0% of the time, Pallas kernels for 0%

profile of v4, /device:TPU:1, one launch (start us, length us, event | category | flops | bytes accessed | tf_op | source)
XLA Modules:
  0.0 66.7 jit_solution(10230738942377048134)
XLA Ops:
  0.6 0.0 copy-start.3
  0.6 0.0 copy-start.4
  0.7 0.0 copy-start.8
  0.7 0.0 copy-start.9
  0.7 1.2 %gate.1 = f32[768,128]{1,0:T(8,128)S(1)} custom-call(bf16[32,1024]{1,0:T(8,128)(2,1)} %grad_out.1, bf16[32,1024]{1,0:T(8,128)(2,1)} %refs_1_.2, bf16[32,1024]{1,0:T(8,128)(2,1)} %key_proj.1, bf16[32,1024]{1,0:T(8,128)(2,1)} %value.1, f32[32,1024]{1,0:T(8,128)} %refs_4_.2), custom_call_target="tpu_custom_call" | custom-call | tf_op jit(solution)/shard_map/gate/pallas_call | solution.py:163
  1.9 0.0 copy-start
  1.9 0.0 copy-start.1
  1.9 0.0 copy-start.2
  1.9 27.9 %all_to_all.15.refs_0_ = f32[32,24,128]{2,1,0:T(8,128)S(1)} all-to-all(f32[32,24,128]{2,1,0:T(8,128)S(1)} %bitcast.4), channel_id=1, replica_groups=mesh['ctx'=32,'chan'=8] {'ctx'}, dimensions={0} | all-to-all | bytes 786432 | tf_op jit(solution)/shard_map/all_to_all | solution.py:172
  29.7 0.0 copy-done.4
  29.8 2.4 %spectral.1 = (f32[32,16,128]{2,1,0:T(8,128)}, f32[32,8,128]{2,1,0:T(8,128)S(1)}) custom-call(f32[32,24,128]{2,1,0:T(8,128)S(1)} %all_to_all.15.refs_0_, bf16[512,256]{1,0:T(8,128)(2,1)S(1)} %copy-done.4, bf16[512,256]{1,0:T(8,128)(2,1)S(1)} %copy-done.3, bf16[256,256]{1,0:T(8,128)(2,1)S(1)} %copy-done.9, bf16[256,256]{1,0:T(8,128)(2,1)S(1)} %copy-done.8, ...), custom_call_target="tpu_custom_call" | custom-call | tf_op jit(solution)/shard_map/spectral/pallas_call | solution.py:174
  32.2 15.1 %all_to_all.16 = f32[32,8,128]{2,1,0:T(8,128)S(1)} all-to-all(f32[32,8,128]{2,1,0:T(8,128)S(1)} %get-tuple-element.7), channel_id=1, replica_groups=mesh['ctx'=32,'chan'=8] {'ctx'}, dimensions={0} | all-to-all | bytes 262144 | tf_op jit(solution)/shard_map/all_to_all | solution.py:185
  47.3 1.3 %collective-permute-start = (f32[256,128]{1,0:T(8,128)S(1)}, f32[256,128]{1,0:T(8,128)S(1)}, u32[]{:S(2)}, u32[]{:S(2)}) collective-permute-start(f32[256,128]{1,0:T(8,128)S(1)} %bitcast.6), channel_id=1, source_target_pairs={{0,2},{1,3},{2,0},{3,1},{4,6},{5,7},{6,4},{7,5},{8,10},{9,11},{10,... | collective-permute-start | bytes 393224 | tf_op jit(solution)/shard_map/ppermute | solution.py:187
  48.6 4.0 %all-to-all-start.1 = ((f32[32,16,128]{2,1,0:T(8,128)}), f32[32,16,128]{2,1,0:T(8,128)S(1)}, u32[]{:S(2)}, u32[]{:S(2)}) async-start(f32[32,16,128]{2,1,0:T(8,128)} %get-tuple-element.6), calls=%async_computation.1 | async-start | bytes 524288 | tf_op jit(solution)/shard_map/all_to_all | solution.py:186
  52.6 0.0 collective-permute-done
  52.6 0.0 copy-start.5
  52.6 0.0 copy-start.6
  52.6 0.0 copy-start.7
  52.6 2.5 %collective-permute-start.1 = (f32[256,128]{1,0:T(8,128)S(1)}, f32[256,128]{1,0:T(8,128)S(1)}, u32[]{:S(2)}, u32[]{:S(2)}) collective-permute-start(f32[256,128]{1,0:T(8,128)S(1)} %bitcast_add_fusion), channel_id=1, source_target_pairs={{0,6},{1,7},{2,4},{3,5},{4,2},{5,3},{6,0},{7,1},{8,14},{9,15},{10,... | collective-permute-start | bytes 393224 | tf_op jit(solution)/shard_map/ppermute | solution.py:188
  55.1 3.2 %collective-permute-done.1 = f32[256,128]{1,0:T(8,128)S(1)} collective-permute-done((f32[256,128]{1,0:T(8,128)S(1)}, f32[256,128]{1,0:T(8,128)S(1)}, u32[]{:S(2)}, u32[]{:S(2)}) %collective-permute-start.1) | collective-permute-done | bytes 131104 | tf_op jit(solution)/shard_map/ppermute | solution.py:188
  58.4 1.1 %collective-permute-start.2 = (f32[256,128]{1,0:T(8,128)S(1)}, f32[256,128]{1,0:T(8,128)S(1)}, u32[]{:S(2)}, u32[]{:S(2)}) collective-permute-start(f32[256,128]{1,0:T(8,128)S(1)} %add.7.total), channel_id=1, source_target_pairs={{0,1},{1,0},{2,3},{3,2},{4,5},{5,4},{6,7},{7,6},{8,9},{9,8},{10,11... | collective-permute-start | bytes 393224 | tf_op jit(solution)/shard_map/ppermute | solution.py:189
  59.5 6.3 %all-to-all-done.1 = f32[32,16,128]{2,1,0:T(8,128)S(1)} async-done(((f32[32,16,128]{2,1,0:T(8,128)}), f32[32,16,128]{2,1,0:T(8,128)S(1)}, u32[]{:S(2)}, u32[]{:S(2)}) %all-to-all-start.1) | async-done | bytes 262176 | tf_op jit(solution)/shard_map/all_to_all | solution.py:186
  65.8 0.0 collective-permute-done.2.swapped
  65.8 0.9 %grads.1 = (bf16[32,1024]{1,0:T(8,128)(2,1)}, bf16[32,1024]{1,0:T(8,128)(2,1)}, bf16[32,1024]{1,0:T(8,128)(2,1)}, f32[32,1024]{1,0:T(8,128)}) custom-call(f32[512,128]{1,0:T(8,128)S(1)} %bitcast.5, bf16[32,1024]{1,0:T(8,128)(2,1)S(1)} %copy-done.5, bf16[32,1024]{1,0:T(8,128)(2,1)S(1)} %copy-done.6, bf16[32,1024]{1,0:T(8,128)(2,1)S(1)} %copy-done.7, ...), custom_call_target="tpu_custom_call" | custom-call | tf_op jit(solution)/shard_map/grads/pallas_call | solution.py:190
  (11 shorter events, 0.1 us)
Async XLA Ops:
  0.6 29.1 %copy-start.3 = (bf16[512,256]{1,0:T(8,128)(2,1)S(1)}, bf16[512,256]{1,0:T(8,128)(2,1)}, u32[]{:S(2)}) copy-start(bf16[512,256]{1,0:T(8,128)(2,1)} %constant.15.clone.refs_2_) | copy-start | bytes 786436
  0.6 29.1 %copy-start.4 = (bf16[512,256]{1,0:T(8,128)(2,1)S(1)}, bf16[512,256]{1,0:T(8,128)(2,1)}, u32[]{:S(2)}) copy-start(bf16[512,256]{1,0:T(8,128)(2,1)} %constant.14.clone.refs_1_) | copy-start | bytes 786436
  0.7 29.1 %copy-start.8 = (bf16[256,256]{1,0:T(8,128)(2,1)S(1)}, bf16[256,256]{1,0:T(8,128)(2,1)}, u32[]{:S(2)}) copy-start(bf16[256,256]{1,0:T(8,128)(2,1)} %constant.17.clone.refs_4_) | copy-start | bytes 393220
  0.7 29.1 %copy-start.9 = (bf16[256,256]{1,0:T(8,128)(2,1)S(1)}, bf16[256,256]{1,0:T(8,128)(2,1)}, u32[]{:S(2)}) copy-start(bf16[256,256]{1,0:T(8,128)(2,1)} %constant.16.clone.refs_3_) | copy-start | bytes 393220
  1.9 27.9 %copy-start = (f32[256,256]{1,0:T(8,128)S(1)}, f32[256,256]{1,0:T(8,128)}, u32[]{:S(2)}) copy-start(f32[256,256]{1,0:T(8,128)} %constant.20.clone.refs_7_) | copy-start | bytes 786436
  1.9 27.9 %copy-start.1 = (bf16[256,512]{1,0:T(8,128)(2,1)S(1)}, bf16[256,512]{1,0:T(8,128)(2,1)}, u32[]{:S(2)}) copy-start(bf16[256,512]{1,0:T(8,128)(2,1)} %constant.19.clone.refs_6_) | copy-start | bytes 786436
  1.9 27.9 %copy-start.2 = (bf16[256,512]{1,0:T(8,128)(2,1)S(1)}, bf16[256,512]{1,0:T(8,128)(2,1)}, u32[]{:S(2)}) copy-start(bf16[256,512]{1,0:T(8,128)(2,1)} %constant.18.clone.refs_5_) | copy-start | bytes 786436
  47.3 5.3 %collective-permute-start = (f32[256,128]{1,0:T(8,128)S(1)}, f32[256,128]{1,0:T(8,128)S(1)}, u32[]{:S(2)}, u32[]{:S(2)}) collective-permute-start(f32[256,128]{1,0:T(8,128)S(1)} %bitcast.6), channel_id=1, source_target_pairs={{0,2},{1,3},{2,0},{3,1},{4,6},{5,7},{6,4},{7,5},{8,10},{9,11},{10,... | collective-permute-start | bytes 393224 | tf_op jit(solution)/shard_map/ppermute | solution.py:187
  48.6 17.2 %all-to-all-start.1 = ((f32[32,16,128]{2,1,0:T(8,128)}), f32[32,16,128]{2,1,0:T(8,128)S(1)}, u32[]{:S(2)}, u32[]{:S(2)}) async-start(f32[32,16,128]{2,1,0:T(8,128)} %get-tuple-element.6), calls=%async_computation.1 | async-start | bytes 524288 | tf_op jit(solution)/shard_map/all_to_all | solution.py:186
  52.6 13.2 %copy-start.5 = (bf16[32,1024]{1,0:T(8,128)(2,1)S(1)}, bf16[32,1024]{1,0:T(8,128)(2,1)}, u32[]{:S(2)}) copy-start(bf16[32,1024]{1,0:T(8,128)(2,1)} %grad_out.1) | copy-start | bytes 196612
  52.6 13.2 %copy-start.6 = (bf16[32,1024]{1,0:T(8,128)(2,1)S(1)}, bf16[32,1024]{1,0:T(8,128)(2,1)}, u32[]{:S(2)}) copy-start(bf16[32,1024]{1,0:T(8,128)(2,1)} %key_proj.1) | copy-start | bytes 196612
  52.6 13.2 %copy-start.7 = (bf16[32,1024]{1,0:T(8,128)(2,1)S(1)}, bf16[32,1024]{1,0:T(8,128)(2,1)}, u32[]{:S(2)}) copy-start(bf16[32,1024]{1,0:T(8,128)(2,1)} %value.1) | copy-start | bytes 196612
  52.6 5.7 %collective-permute-start.1 = (f32[256,128]{1,0:T(8,128)S(1)}, f32[256,128]{1,0:T(8,128)S(1)}, u32[]{:S(2)}, u32[]{:S(2)}) collective-permute-start(f32[256,128]{1,0:T(8,128)S(1)} %bitcast_add_fusion), channel_id=1, source_target_pairs={{0,6},{1,7},{2,4},{3,5},{4,2},{5,3},{6,0},{7,1},{8,14},{9,15},{10,... | collective-permute-start | bytes 393224 | tf_op jit(solution)/shard_map/ppermute | solution.py:188
  58.4 7.4 %collective-permute-start.2 = (f32[256,128]{1,0:T(8,128)S(1)}, f32[256,128]{1,0:T(8,128)S(1)}, u32[]{:S(2)}, u32[]{:S(2)}) collective-permute-start(f32[256,128]{1,0:T(8,128)S(1)} %add.7.total), channel_id=1, source_target_pairs={{0,1},{1,0},{2,3},{3,2},{4,5},{5,4},{6,7},{7,6},{8,9},{9,8},{10,11... | collective-permute-start | bytes 393224 | tf_op jit(solution)/shard_map/ppermute | solution.py:189

commit v5 on v4

--- a/solution.py
+++ b/solution.py
@@ -184,9 +184,12 @@
     )(taken, *tables)
     partial = lax.all_to_all(corr, "ctx", 0, 0, tiled=True).reshape(channels * pieces, LANES)
     back = lax.all_to_all(timed, "ctx", 0, 0, tiled=True)
-    total = partial + lax.ppermute(partial, "chan", [(i, i ^ 2) for i in range(groups)])
-    total = total + lax.ppermute(total, "chan", [(i, 2 * (groups // 2 - 1 - i // 2) + i % 2) for i in range(groups)])
-    swapped = lax.ppermute(total, "chan", [(i, i ^ 1) for i in range(groups)])
+    def moved(values, bit):
+        return lax.ppermute(values, "chan", [(i, i ^ bit) for i in range(groups)])
+
+    total = partial + moved(partial, 1)
+    total = total + moved(total, 2)
+    swapped = moved(total, 4)
     grad_query, grad_key, grad_value, grad_filter = pl.pallas_call(
         grads_kernel,
         out_shape=[jax.ShapeDtypeStruct((channels, here), jnp.bfloat16)] * 3

time: 66.9 us -> 66.4 us (level)
  transfers between devices with their start and end apart: 4 -> 4, of which waited for: 2 -> 3; matrix products, arithmetic and copies ran while one was open for 0% -> 0% of each run, Pallas kernels for 0% -> 0%
where the time goes in v5:
time: 66.4 us; the launch traced here: 66.2 us
  blocking collectives  43 us (65%)
  waiting for transfers between devices  9.03 us (14%)
  starting transfers between devices  8.88 us (13%)
  Pallas kernels  4.41 us (7%)
  between operations  0.79 us (1%)
    all_to_all x1, blocking collectives, local(): lax.all_to_all(gated.reshape(channels, 3 * pieces, LANES), 'ctx', 0, 0, t...  27.9 us
    all_to_all x1, blocking collectives, local(): lax.all_to_all(corr, 'ctx', 0, 0, tiled=True)  15.1 us
    all_to_all x1, waiting for transfers between devices, local(): back = lax.all_to_all(timed, 'ctx', 0, 0, tiled=True)  5.76 us
    ppermute x3, starting transfers between devices, moved(): return lax.ppermute(values, 'chan', [(i, i ^ bit) for i in range(groups)])  5.23 us
    all_to_all x1, starting transfers between devices, local(): back = lax.all_to_all(timed, 'ctx', 0, 0, tiled=True)  3.65 us
    ppermute x3, waiting for transfers between devices, moved(): return lax.ppermute(values, 'chan', [(i, i ^ bit) for i in range(groups)])  3.27 us
    pallas_call x1, Pallas kernels, local(): pl.pallas_call(lambda *refs: spectral_kernel(*refs, filter_scale=filter_s...  2.38 us
  transfers between devices with their start and end apart: 4, of which 3 were waited for; matrix products, arithmetic and copies ran while one was open for 0% of the time, Pallas kernels for 0%

profile of v5, /device:TPU:1, one launch (start us, length us, event | category | flops | bytes accessed | tf_op | source)
XLA Modules:
  0.0 66.2 jit_solution(10138367361067250628)
XLA Ops:
  0.6 0.0 copy-start.3
  0.6 0.0 copy-start.4
  0.7 0.0 copy-start.8
  0.7 0.0 copy-start.9
  0.7 1.2 %gate.1 = f32[768,128]{1,0:T(8,128)S(1)} custom-call(bf16[32,1024]{1,0:T(8,128)(2,1)} %grad_out.1, bf16[32,1024]{1,0:T(8,128)(2,1)} %refs_1_.2, bf16[32,1024]{1,0:T(8,128)(2,1)} %key_proj.1, bf16[32,1024]{1,0:T(8,128)(2,1)} %value.1, f32[32,1024]{1,0:T(8,128)} %refs_4_.2), custom_call_target="tpu_custom_call" | custom-call | tf_op jit(solution)/shard_map/gate/pallas_call | solution.py:163
  1.9 0.0 copy-start
  1.9 0.0 copy-start.1
  1.9 0.0 copy-start.2
  1.9 27.9 %all_to_all.15.refs_0_ = f32[32,24,128]{2,1,0:T(8,128)S(1)} all-to-all(f32[32,24,128]{2,1,0:T(8,128)S(1)} %bitcast.4), channel_id=1, replica_groups=mesh['ctx'=32,'chan'=8] {'ctx'}, dimensions={0} | all-to-all | bytes 786432 | tf_op jit(solution)/shard_map/all_to_all | solution.py:172
  29.7 0.0 copy-done.3
  29.8 2.4 %spectral.1 = (f32[32,16,128]{2,1,0:T(8,128)}, f32[32,8,128]{2,1,0:T(8,128)S(1)}) custom-call(f32[32,24,128]{2,1,0:T(8,128)S(1)} %all_to_all.15.refs_0_, bf16[512,256]{1,0:T(8,128)(2,1)S(1)} %copy-done.4, bf16[512,256]{1,0:T(8,128)(2,1)S(1)} %copy-done.3, bf16[256,256]{1,0:T(8,128)(2,1)S(1)} %copy-done.9, bf16[256,256]{1,0:T(8,128)(2,1)S(1)} %copy-done.8, ...), custom_call_target="tpu_custom_call" | custom-call | tf_op jit(solution)/shard_map/spectral/pallas_call | solution.py:174
  32.2 15.1 %all_to_all.16 = f32[32,8,128]{2,1,0:T(8,128)S(1)} all-to-all(f32[32,8,128]{2,1,0:T(8,128)S(1)} %get-tuple-element.7), channel_id=1, replica_groups=mesh['ctx'=32,'chan'=8] {'ctx'}, dimensions={0} | all-to-all | bytes 262144 | tf_op jit(solution)/shard_map/all_to_all | solution.py:185
  47.3 0.8 %collective-permute-start = (f32[256,128]{1,0:T(8,128)S(1)}, f32[256,128]{1,0:T(8,128)S(1)}, u32[]{:S(2)}, u32[]{:S(2)}) collective-permute-start(f32[256,128]{1,0:T(8,128)S(1)} %bitcast.6), channel_id=1, source_target_pairs={{0,1},{1,0},{2,3},{3,2},{4,5},{5,4},{6,7},{7,6},{8,9},{9,8},{10,11... | collective-permute-start | bytes 393224 | tf_op jit(solution)/shard_map/ppermute | solution.py:188
  48.1 3.7 %all-to-all-start.1 = ((f32[32,16,128]{2,1,0:T(8,128)}), f32[32,16,128]{2,1,0:T(8,128)S(1)}, u32[]{:S(2)}, u32[]{:S(2)}) async-start(f32[32,16,128]{2,1,0:T(8,128)} %get-tuple-element.6), calls=%async_computation.1 | async-start | bytes 524288 | tf_op jit(solution)/shard_map/all_to_all | solution.py:186
  51.8 0.5 collective-permute-done
  52.3 0.0 copy-start.5
  52.3 0.0 copy-start.6
  52.3 0.0 copy-start.7
  52.3 1.4 %collective-permute-start.1 = (f32[256,128]{1,0:T(8,128)S(1)}, f32[256,128]{1,0:T(8,128)S(1)}, u32[]{:S(2)}, u32[]{:S(2)}) collective-permute-start(f32[256,128]{1,0:T(8,128)S(1)} %bitcast_add_fusion), channel_id=1, source_target_pairs={{0,2},{1,3},{2,0},{3,1},{4,6},{5,7},{6,4},{7,5},{8,10},{9,11},{10,... | collective-permute-start | bytes 393224 | tf_op jit(solution)/shard_map/ppermute | solution.py:188
  53.7 2.8 %collective-permute-done.1 = f32[256,128]{1,0:T(8,128)S(1)} collective-permute-done((f32[256,128]{1,0:T(8,128)S(1)}, f32[256,128]{1,0:T(8,128)S(1)}, u32[]{:S(2)}, u32[]{:S(2)}) %collective-permute-start.1) | collective-permute-done | bytes 131104 | tf_op jit(solution)/shard_map/ppermute | solution.py:188
  56.5 3.0 %collective-permute-start.2 = (f32[256,128]{1,0:T(8,128)S(1)}, f32[256,128]{1,0:T(8,128)S(1)}, u32[]{:S(2)}, u32[]{:S(2)}) collective-permute-start(f32[256,128]{1,0:T(8,128)S(1)} %add.7.total), channel_id=1, source_target_pairs={{0,4},{1,5},{2,6},{3,7},{4,0},{5,1},{6,2},{7,3},{8,12},{9,13},{10,... | collective-permute-start | bytes 393224 | tf_op jit(solution)/shard_map/ppermute | solution.py:188
  59.5 5.8 %all-to-all-done.1 = f32[32,16,128]{2,1,0:T(8,128)S(1)} async-done(((f32[32,16,128]{2,1,0:T(8,128)}), f32[32,16,128]{2,1,0:T(8,128)S(1)}, u32[]{:S(2)}, u32[]{:S(2)}) %all-to-all-start.1) | async-done | bytes 262176 | tf_op jit(solution)/shard_map/all_to_all | solution.py:186
  65.3 0.0 collective-permute-done.2.swapped
  65.3 0.9 %grads.1 = (bf16[32,1024]{1,0:T(8,128)(2,1)}, bf16[32,1024]{1,0:T(8,128)(2,1)}, bf16[32,1024]{1,0:T(8,128)(2,1)}, f32[32,1024]{1,0:T(8,128)}) custom-call(f32[512,128]{1,0:T(8,128)S(1)} %bitcast.5, bf16[32,1024]{1,0:T(8,128)(2,1)S(1)} %copy-done.5, bf16[32,1024]{1,0:T(8,128)(2,1)S(1)} %copy-done.6, bf16[32,1024]{1,0:T(8,128)(2,1)S(1)} %copy-done.7, ...), custom_call_target="tpu_custom_call" | custom-call | tf_op jit(solution)/shard_map/grads/pallas_call | solution.py:193
  (11 shorter events, 0.0 us)
Async XLA Ops:
  0.6 29.1 %copy-start.3 = (bf16[512,256]{1,0:T(8,128)(2,1)S(1)}, bf16[512,256]{1,0:T(8,128)(2,1)}, u32[]{:S(2)}) copy-start(bf16[512,256]{1,0:T(8,128)(2,1)} %constant.15.clone.refs_2_) | copy-start | bytes 786436
  0.6 29.1 %copy-start.4 = (bf16[512,256]{1,0:T(8,128)(2,1)S(1)}, bf16[512,256]{1,0:T(8,128)(2,1)}, u32[]{:S(2)}) copy-start(bf16[512,256]{1,0:T(8,128)(2,1)} %constant.14.clone.refs_1_) | copy-start | bytes 786436
  0.7 29.1 %copy-start.8 = (bf16[256,256]{1,0:T(8,128)(2,1)S(1)}, bf16[256,256]{1,0:T(8,128)(2,1)}, u32[]{:S(2)}) copy-start(bf16[256,256]{1,0:T(8,128)(2,1)} %constant.17.clone.refs_4_) | copy-start | bytes 393220
  0.7 29.1 %copy-start.9 = (bf16[256,256]{1,0:T(8,128)(2,1)S(1)}, bf16[256,256]{1,0:T(8,128)(2,1)}, u32[]{:S(2)}) copy-start(bf16[256,256]{1,0:T(8,128)(2,1)} %constant.16.clone.refs_3_) | copy-start | bytes 393220
  1.9 27.9 %copy-start = (f32[256,256]{1,0:T(8,128)S(1)}, f32[256,256]{1,0:T(8,128)}, u32[]{:S(2)}) copy-start(f32[256,256]{1,0:T(8,128)} %constant.20.clone.refs_7_) | copy-start | bytes 786436
  1.9 27.9 %copy-start.1 = (bf16[256,512]{1,0:T(8,128)(2,1)S(1)}, bf16[256,512]{1,0:T(8,128)(2,1)}, u32[]{:S(2)}) copy-start(bf16[256,512]{1,0:T(8,128)(2,1)} %constant.19.clone.refs_6_) | copy-start | bytes 786436
  1.9 27.9 %copy-start.2 = (bf16[256,512]{1,0:T(8,128)(2,1)S(1)}, bf16[256,512]{1,0:T(8,128)(2,1)}, u32[]{:S(2)}) copy-start(bf16[256,512]{1,0:T(8,128)(2,1)} %constant.18.clone.refs_5_) | copy-start | bytes 786436
  47.3 5.0 %collective-permute-start = (f32[256,128]{1,0:T(8,128)S(1)}, f32[256,128]{1,0:T(8,128)S(1)}, u32[]{:S(2)}, u32[]{:S(2)}) collective-permute-start(f32[256,128]{1,0:T(8,128)S(1)} %bitcast.6), channel_id=1, source_target_pairs={{0,1},{1,0},{2,3},{3,2},{4,5},{5,4},{6,7},{7,6},{8,9},{9,8},{10,11... | collective-permute-start | bytes 393224 | tf_op jit(solution)/shard_map/ppermute | solution.py:188
  48.1 17.1 %all-to-all-start.1 = ((f32[32,16,128]{2,1,0:T(8,128)}), f32[32,16,128]{2,1,0:T(8,128)S(1)}, u32[]{:S(2)}, u32[]{:S(2)}) async-start(f32[32,16,128]{2,1,0:T(8,128)} %get-tuple-element.6), calls=%async_computation.1 | async-start | bytes 524288 | tf_op jit(solution)/shard_map/all_to_all | solution.py:186
  52.3 13.0 %copy-start.5 = (bf16[32,1024]{1,0:T(8,128)(2,1)S(1)}, bf16[32,1024]{1,0:T(8,128)(2,1)}, u32[]{:S(2)}) copy-start(bf16[32,1024]{1,0:T(8,128)(2,1)} %grad_out.1) | copy-start | bytes 196612
  52.3 13.0 %copy-start.6 = (bf16[32,1024]{1,0:T(8,128)(2,1)S(1)}, bf16[32,1024]{1,0:T(8,128)(2,1)}, u32[]{:S(2)}) copy-start(bf16[32,1024]{1,0:T(8,128)(2,1)} %key_proj.1) | copy-start | bytes 196612
  52.3 13.0 %copy-start.7 = (bf16[32,1024]{1,0:T(8,128)(2,1)S(1)}, bf16[32,1024]{1,0:T(8,128)(2,1)}, u32[]{:S(2)}) copy-start(bf16[32,1024]{1,0:T(8,128)(2,1)} %value.1) | copy-start | bytes 196612
  52.3 4.2 %collective-permute-start.1 = (f32[256,128]{1,0:T(8,128)S(1)}, f32[256,128]{1,0:T(8,128)S(1)}, u32[]{:S(2)}, u32[]{:S(2)}) collective-permute-start(f32[256,128]{1,0:T(8,128)S(1)} %bitcast_add_fusion), channel_id=1, source_target_pairs={{0,2},{1,3},{2,0},{3,1},{4,6},{5,7},{6,4},{7,5},{8,10},{9,11},{10,... | collective-permute-start | bytes 393224 | tf_op jit(solution)/shard_map/ppermute | solution.py:188
  56.5 8.8 %collective-permute-start.2 = (f32[256,128]{1,0:T(8,128)S(1)}, f32[256,128]{1,0:T(8,128)S(1)}, u32[]{:S(2)}, u32[]{:S(2)}) collective-permute-start(f32[256,128]{1,0:T(8,128)S(1)} %add.7.total), channel_id=1, source_target_pairs={{0,4},{1,5},{2,6},{3,7},{4,0},{5,1},{6,2},{7,3},{8,12},{9,13},{10,... | collective-permute-start | bytes 393224 | tf_op jit(solution)/shard_map/ppermute | solution.py:188

commit v6 on v5

--- a/solution.py
+++ b/solution.py
@@ -135,20 +135,34 @@
 
 
 def grads_kernel(
-    back, grad_out, key_proj, value, total, swapped, grad_query, grad_key, grad_value, grad_filter
+    back, grad_out, key_proj, value, total, swapped, grad_query, grad_key, grad_value, grad_filter, gq, gk, gv, gf, sems
 ):
     f32 = jnp.float32
     channels, here = key_proj.shape
     pieces = here // LANES
-    for piece in range(pieces):
-        columns = slice(piece * LANES, (piece + 1) * LANES)
+    blocks = [slice(piece * LANES, (piece + 1) * LANES) for piece in range(pieces)]
+    copies = []
+
+    def send(held, target):
+        copies.append(pltpu.make_async_copy(held, target, sems.at[len(copies)]))
+        copies[-1].start()
+
+    for piece, columns in enumerate(blocks):
         rows = pl.ds(piece, channels, stride=pieces)
-        grad_filter[:, columns] = total[rows, :] + swapped[rows, :]
+        gf[:, columns] = total[rows, :] + swapped[rows, :]
+    send(gf, grad_filter)
+    for piece, columns in enumerate(blocks):
         conv = back[pl.ds(piece, channels, stride=2 * pieces), :]
+        gq[:, columns] = (grad_out[:, columns].astype(f32) * conv).astype(jnp.bfloat16)
+    send(gq, grad_query)
+    for piece, columns in enumerate(blocks):
         grad_signal = back[pl.ds(pieces + piece, channels, stride=2 * pieces), :]
-        grad_query[:, columns] = (grad_out[:, columns].astype(f32) * conv).astype(jnp.bfloat16)
-        grad_key[:, columns] = (grad_signal * value[:, columns].astype(f32)).astype(jnp.bfloat16)
-        grad_value[:, columns] = (grad_signal * key_proj[:, columns].astype(f32)).astype(jnp.bfloat16)
+        gk[:, columns] = (grad_signal * value[:, columns].astype(f32)).astype(jnp.bfloat16)
+        gv[:, columns] = (grad_signal * key_proj[:, columns].astype(f32)).astype(jnp.bfloat16)
+    send(gk, grad_key)
+    send(gv, grad_value)
+    for copy in copies:
+        copy.wait()
 
 
 def local(grad_out, query, key_proj, value, filter_param):
@@ -194,6 +208,9 @@
         grads_kernel,
         out_shape=[jax.ShapeDtypeStruct((channels, here), jnp.bfloat16)] * 3
         + [jax.ShapeDtypeStruct((channels, here), f32)],
+        out_specs=[pl.BlockSpec(memory_space=pltpu.HBM)] * 4,
+        scratch_shapes=[pltpu.VMEM((channels, here), jnp.bfloat16)] * 3
+        + [pltpu.VMEM((channels, here), f32), pltpu.SemaphoreType.DMA((4,))],
         compiler_params=params,
         name="grads",
     )(back.reshape(channels * 2 * pieces, LANES), grad_out, key_proj, value, total, swapped)

time: 66.4 us -> 66.4 us (level)
  no operation moved by 1% of the time
where the time goes in v6:
time: 66.4 us; the launch traced here: 66.1 us
  blocking collectives  43 us (65%)
  waiting for transfers between devices  9.03 us (14%)
  starting transfers between devices  8.88 us (13%)
  Pallas kernels  4.36 us (7%)
  between operations  0.79 us (1%)
    all_to_all x1, blocking collectives, local(): lax.all_to_all(gated.reshape(channels, 3 * pieces, LANES), 'ctx', 0, 0, t...  27.9 us
    all_to_all x1, blocking collectives, local(): lax.all_to_all(corr, 'ctx', 0, 0, tiled=True)  15.1 us
    all_to_all x1, waiting for transfers between devices, local(): back = lax.all_to_all(timed, 'ctx', 0, 0, tiled=True)  5.76 us
    ppermute x3, starting transfers between devices, moved(): return lax.ppermute(values, 'chan', [(i, i ^ bit) for i in range(groups)])  5.23 us
    all_to_all x1, starting transfers between devices, local(): back = lax.all_to_all(timed, 'ctx', 0, 0, tiled=True)  3.65 us
    ppermute x3, waiting for transfers between devices, moved(): return lax.ppermute(values, 'chan', [(i, i ^ bit) for i in range(groups)])  3.27 us
    pallas_call x1, Pallas kernels, local(): pl.pallas_call(lambda *refs: spectral_kernel(*refs, filter_scale=filter_s...  2.38 us
  transfers between devices with their start and end apart: 4, of which 3 were waited for; matrix products, arithmetic and copies ran while one was open for 0% of the time, Pallas kernels for 0%

profile of v6, /device:TPU:1, one launch (start us, length us, event | category | flops | bytes accessed | tf_op | source)
XLA Modules:
  0.0 66.1 jit_solution(8756236413203362992)
XLA Ops:
  0.6 0.0 copy-start.3
  0.6 0.0 copy-start.4
  0.7 0.0 copy-start.8
  0.7 0.0 copy-start.9
  0.7 1.2 %gate.1 = f32[768,128]{1,0:T(8,128)S(1)} custom-call(bf16[32,1024]{1,0:T(8,128)(2,1)} %grad_out.1, bf16[32,1024]{1,0:T(8,128)(2,1)} %refs_1_.2, bf16[32,1024]{1,0:T(8,128)(2,1)} %key_proj.1, bf16[32,1024]{1,0:T(8,128)(2,1)} %value.1, f32[32,1024]{1,0:T(8,128)} %refs_4_.2), custom_call_target="tpu_custom_call" | custom-call | tf_op jit(solution)/shard_map/gate/pallas_call | solution.py:177
  1.9 0.0 copy-start
  1.9 0.0 copy-start.1
  1.9 0.0 copy-start.2
  1.9 27.9 %all_to_all.15.refs_0_ = f32[32,24,128]{2,1,0:T(8,128)S(1)} all-to-all(f32[32,24,128]{2,1,0:T(8,128)S(1)} %bitcast.4), channel_id=1, replica_groups=mesh['ctx'=32,'chan'=8] {'ctx'}, dimensions={0} | all-to-all | bytes 786432 | tf_op jit(solution)/shard_map/all_to_all | solution.py:186
  29.7 0.0 copy-done.3
  29.8 2.4 %spectral.1 = (f32[32,16,128]{2,1,0:T(8,128)}, f32[32,8,128]{2,1,0:T(8,128)S(1)}) custom-call(f32[32,24,128]{2,1,0:T(8,128)S(1)} %all_to_all.15.refs_0_, bf16[512,256]{1,0:T(8,128)(2,1)S(1)} %copy-done.4, bf16[512,256]{1,0:T(8,128)(2,1)S(1)} %copy-done.3, bf16[256,256]{1,0:T(8,128)(2,1)S(1)} %copy-done.9, bf16[256,256]{1,0:T(8,128)(2,1)S(1)} %copy-done.8, ...), custom_call_target="tpu_custom_call" | custom-call | tf_op jit(solution)/shard_map/spectral/pallas_call | solution.py:188
  32.2 15.1 %all_to_all.16 = f32[32,8,128]{2,1,0:T(8,128)S(1)} all-to-all(f32[32,8,128]{2,1,0:T(8,128)S(1)} %get-tuple-element.7), channel_id=1, replica_groups=mesh['ctx'=32,'chan'=8] {'ctx'}, dimensions={0} | all-to-all | bytes 262144 | tf_op jit(solution)/shard_map/all_to_all | solution.py:199
  47.3 0.8 %collective-permute-start = (f32[256,128]{1,0:T(8,128)S(1)}, f32[256,128]{1,0:T(8,128)S(1)}, u32[]{:S(2)}, u32[]{:S(2)}) collective-permute-start(f32[256,128]{1,0:T(8,128)S(1)} %bitcast.6), channel_id=1, source_target_pairs={{0,1},{1,0},{2,3},{3,2},{4,5},{5,4},{6,7},{7,6},{8,9},{9,8},{10,11... | collective-permute-start | bytes 393224 | tf_op jit(solution)/shard_map/ppermute | solution.py:202
  48.1 3.7 %all-to-all-start.1 = ((f32[32,16,128]{2,1,0:T(8,128)}), f32[32,16,128]{2,1,0:T(8,128)S(1)}, u32[]{:S(2)}, u32[]{:S(2)}) async-start(f32[32,16,128]{2,1,0:T(8,128)} %get-tuple-element.6), calls=%async_computation.1 | async-start | bytes 524288 | tf_op jit(solution)/shard_map/all_to_all | solution.py:200
  51.8 0.5 collective-permute-done
  52.3 0.0 copy-start.5
  52.3 0.0 copy-start.6
  52.3 0.0 copy-start.7
  52.3 1.4 %collective-permute-start.1 = (f32[256,128]{1,0:T(8,128)S(1)}, f32[256,128]{1,0:T(8,128)S(1)}, u32[]{:S(2)}, u32[]{:S(2)}) collective-permute-start(f32[256,128]{1,0:T(8,128)S(1)} %bitcast_add_fusion), channel_id=1, source_target_pairs={{0,2},{1,3},{2,0},{3,1},{4,6},{5,7},{6,4},{7,5},{8,10},{9,11},{10,... | collective-permute-start | bytes 393224 | tf_op jit(solution)/shard_map/ppermute | solution.py:202
  53.7 2.8 %collective-permute-done.1 = f32[256,128]{1,0:T(8,128)S(1)} collective-permute-done((f32[256,128]{1,0:T(8,128)S(1)}, f32[256,128]{1,0:T(8,128)S(1)}, u32[]{:S(2)}, u32[]{:S(2)}) %collective-permute-start.1) | collective-permute-done | bytes 131104 | tf_op jit(solution)/shard_map/ppermute | solution.py:202
  56.5 3.0 %collective-permute-start.2 = (f32[256,128]{1,0:T(8,128)S(1)}, f32[256,128]{1,0:T(8,128)S(1)}, u32[]{:S(2)}, u32[]{:S(2)}) collective-permute-start(f32[256,128]{1,0:T(8,128)S(1)} %add.7.total), channel_id=1, source_target_pairs={{0,4},{1,5},{2,6},{3,7},{4,0},{5,1},{6,2},{7,3},{8,12},{9,13},{10,... | collective-permute-start | bytes 393224 | tf_op jit(solution)/shard_map/ppermute | solution.py:202
  59.5 5.8 %all-to-all-done.1 = f32[32,16,128]{2,1,0:T(8,128)S(1)} async-done(((f32[32,16,128]{2,1,0:T(8,128)}), f32[32,16,128]{2,1,0:T(8,128)S(1)}, u32[]{:S(2)}, u32[]{:S(2)}) %all-to-all-start.1) | async-done | bytes 262176 | tf_op jit(solution)/shard_map/all_to_all | solution.py:200
  65.3 0.0 collective-permute-done.2.swapped
  65.3 0.8 %grads.1 = (bf16[32,1024]{1,0:T(8,128)(2,1)}, bf16[32,1024]{1,0:T(8,128)(2,1)}, bf16[32,1024]{1,0:T(8,128)(2,1)}, f32[32,1024]{1,0:T(8,128)}) custom-call(f32[512,128]{1,0:T(8,128)S(1)} %bitcast.5, bf16[32,1024]{1,0:T(8,128)(2,1)S(1)} %copy-done.5, bf16[32,1024]{1,0:T(8,128)(2,1)S(1)} %copy-done.6, bf16[32,1024]{1,0:T(8,128)(2,1)S(1)} %copy-done.7, ...), custom_call_target="tpu_custom_call" | custom-call | tf_op jit(solution)/shard_map/grads/pallas_call | solution.py:207
  (11 shorter events, 0.0 us)
Async XLA Ops:
  0.6 29.1 %copy-start.3 = (bf16[512,256]{1,0:T(8,128)(2,1)S(1)}, bf16[512,256]{1,0:T(8,128)(2,1)}, u32[]{:S(2)}) copy-start(bf16[512,256]{1,0:T(8,128)(2,1)} %constant.15.clone.refs_2_) | copy-start | bytes 786436
  0.6 29.1 %copy-start.4 = (bf16[512,256]{1,0:T(8,128)(2,1)S(1)}, bf16[512,256]{1,0:T(8,128)(2,1)}, u32[]{:S(2)}) copy-start(bf16[512,256]{1,0:T(8,128)(2,1)} %constant.14.clone.refs_1_) | copy-start | bytes 786436
  0.7 29.1 %copy-start.8 = (bf16[256,256]{1,0:T(8,128)(2,1)S(1)}, bf16[256,256]{1,0:T(8,128)(2,1)}, u32[]{:S(2)}) copy-start(bf16[256,256]{1,0:T(8,128)(2,1)} %constant.17.clone.refs_4_) | copy-start | bytes 393220
  0.7 29.1 %copy-start.9 = (bf16[256,256]{1,0:T(8,128)(2,1)S(1)}, bf16[256,256]{1,0:T(8,128)(2,1)}, u32[]{:S(2)}) copy-start(bf16[256,256]{1,0:T(8,128)(2,1)} %constant.16.clone.refs_3_) | copy-start | bytes 393220
  1.9 27.9 %copy-start = (f32[256,256]{1,0:T(8,128)S(1)}, f32[256,256]{1,0:T(8,128)}, u32[]{:S(2)}) copy-start(f32[256,256]{1,0:T(8,128)} %constant.20.clone.refs_7_) | copy-start | bytes 786436
  1.9 27.9 %copy-start.1 = (bf16[256,512]{1,0:T(8,128)(2,1)S(1)}, bf16[256,512]{1,0:T(8,128)(2,1)}, u32[]{:S(2)}) copy-start(bf16[256,512]{1,0:T(8,128)(2,1)} %constant.19.clone.refs_6_) | copy-start | bytes 786436
  1.9 27.9 %copy-start.2 = (bf16[256,512]{1,0:T(8,128)(2,1)S(1)}, bf16[256,512]{1,0:T(8,128)(2,1)}, u32[]{:S(2)}) copy-start(bf16[256,512]{1,0:T(8,128)(2,1)} %constant.18.clone.refs_5_) | copy-start | bytes 786436
  47.3 5.0 %collective-permute-start = (f32[256,128]{1,0:T(8,128)S(1)}, f32[256,128]{1,0:T(8,128)S(1)}, u32[]{:S(2)}, u32[]{:S(2)}) collective-permute-start(f32[256,128]{1,0:T(8,128)S(1)} %bitcast.6), channel_id=1, source_target_pairs={{0,1},{1,0},{2,3},{3,2},{4,5},{5,4},{6,7},{7,6},{8,9},{9,8},{10,11... | collective-permute-start | bytes 393224 | tf_op jit(solution)/shard_map/ppermute | solution.py:202
  48.1 17.1 %all-to-all-start.1 = ((f32[32,16,128]{2,1,0:T(8,128)}), f32[32,16,128]{2,1,0:T(8,128)S(1)}, u32[]{:S(2)}, u32[]{:S(2)}) async-start(f32[32,16,128]{2,1,0:T(8,128)} %get-tuple-element.6), calls=%async_computation.1 | async-start | bytes 524288 | tf_op jit(solution)/shard_map/all_to_all | solution.py:200
  52.3 13.0 %copy-start.5 = (bf16[32,1024]{1,0:T(8,128)(2,1)S(1)}, bf16[32,1024]{1,0:T(8,128)(2,1)}, u32[]{:S(2)}) copy-start(bf16[32,1024]{1,0:T(8,128)(2,1)} %grad_out.1) | copy-start | bytes 196612
  52.3 13.0 %copy-start.6 = (bf16[32,1024]{1,0:T(8,128)(2,1)S(1)}, bf16[32,1024]{1,0:T(8,128)(2,1)}, u32[]{:S(2)}) copy-start(bf16[32,1024]{1,0:T(8,128)(2,1)} %key_proj.1) | copy-start | bytes 196612
  52.3 13.0 %copy-start.7 = (bf16[32,1024]{1,0:T(8,128)(2,1)S(1)}, bf16[32,1024]{1,0:T(8,128)(2,1)}, u32[]{:S(2)}) copy-start(bf16[32,1024]{1,0:T(8,128)(2,1)} %value.1) | copy-start | bytes 196612
  52.3 4.2 %collective-permute-start.1 = (f32[256,128]{1,0:T(8,128)S(1)}, f32[256,128]{1,0:T(8,128)S(1)}, u32[]{:S(2)}, u32[]{:S(2)}) collective-permute-start(f32[256,128]{1,0:T(8,128)S(1)} %bitcast_add_fusion), channel_id=1, source_target_pairs={{0,2},{1,3},{2,0},{3,1},{4,6},{5,7},{6,4},{7,5},{8,10},{9,11},{10,... | collective-permute-start | bytes 393224 | tf_op jit(solution)/shard_map/ppermute | solution.py:202
  56.5 8.8 %collective-permute-start.2 = (f32[256,128]{1,0:T(8,128)S(1)}, f32[256,128]{1,0:T(8,128)S(1)}, u32[]{:S(2)}, u32[]{:S(2)}) collective-permute-start(f32[256,128]{1,0:T(8,128)S(1)} %add.7.total), channel_id=1, source_target_pairs={{0,4},{1,5},{2,6},{3,7},{4,0},{5,1},{6,2},{7,3},{8,12},{9,13},{10,... | collective-permute-start | bytes 393224 | tf_op jit(solution)/shard_map/ppermute | solution.py:202
